TPU v7x, 32 devices: a whole 2x2x4 slice. The times are simulated.
32 devices in a mesh: seq: 8 (over y, x, core), batch: 4 (over z).
Axes of the slice: x: 2, y: 2, z: 4, core: 2. Of those that a mesh axis runs over, the one named last changes fastest.
Arguments:
- hidden_in: bfloat16 [8, 1024, 768], P('batch', 'seq'), may hold values from -6 to 6
- lengths: int32 [8], P('batch'), may hold values from 1 to 1024, as said below
- attn_weight: bfloat16 [768, 2304], P(('seq', 'batch')), may hold values from -0.21875 to 0.21875
- attn_bias: bfloat16 [2304], P(('seq', 'batch')), may hold values from -0.4375 to 0.4375
- proj_weight: bfloat16 [768, 768], P(('seq', 'batch')), may hold values from -6 to 6
- proj_bias: bfloat16 [768], P(('seq', 'batch')), may hold values from -4 to 4
- first_gain: bfloat16 [768], P(('seq', 'batch')), may hold values from 0.5 to 1.5
- first_shift: bfloat16 [768], P(('seq', 'batch')), may hold values from -4 to 4
- up_weight: bfloat16 [768, 3072], P(('seq', 'batch')), may hold values from -0.21875 to 0.21875
- up_bias: bfloat16 [3072], P(('seq', 'batch')), may hold values from -4 to 4
- down_weight: bfloat16 [3072, 768], P(('seq', 'batch')), may hold values from -0.109375 to 0.109375
- down_bias: bfloat16 [768], P(('seq', 'batch')), may hold values from -4 to 4
- second_gain: bfloat16 [768], P(('seq', 'batch')), may hold values from 0.5 to 1.5
- second_shift: bfloat16 [768], P(('seq', 'batch')), may hold values from -4 to 4
- grad_out: bfloat16 [8, 1024, 768], P('batch', 'seq'), may hold values from -6 to 6
Outputs:
- layer_out: bfloat16 [8, 1024, 768], P('batch', 'seq')
- grad_hidden: float32 [8, 1024, 768], P('batch', 'seq')
- grad_attn_weight: float32 [768, 2304], P(('seq', 'batch'))
- grad_attn_bias: float32 [1536], P(('seq', 'batch'))
- grad_value_bias: float32 [768], P(('seq', 'batch'))
- grad_proj_weight: float32 [768, 768], P(('seq', 'batch'))
- grad_proj_bias: float32 [768], P(('seq', 'batch'))
- grad_first_gain: float32 [768], P(('seq', 'batch'))
- grad_first_shift: float32 [768], P(('seq', 'batch'))
- grad_up_weight: float32 [768, 3072], P(('seq', 'batch'))
- grad_up_bias: float32 [3072], P(('seq', 'batch'))
- grad_down_weight: float32 [3072, 768], P(('seq', 'batch'))
- grad_down_bias: float32 [768], P(('seq', 'batch'))
- grad_second_gain: float32 [768], P(('seq', 'batch'))
- grad_second_shift: float32 [768], P(('seq', 'batch'))
Inputs may be any that keep to these rules, and one draw needn't show every extreme that they name: `lengths`: within the 2 entries of each index of batch at least one equals 1024; some entry equals 1.
All inputs are finite; a program needn't handle non-finite values.
Results may differ from a plain program's by a relative error of at most 0.02.
Values may be sent and summed in bfloat16 or wider, within the bound.
No kernel may reach another device: no remote copies, remote signals or barrier semaphores. Data moves between devices by JAX's collectives and lax.ppermute only.
A program may use at most 128 MiB of HBM per device.

v0:
```python
import jax
import jax.numpy as jnp
from jax import lax
from jax.sharding import PartitionSpec as P

HEADS = 12
HEAD_DIM = 64


EPSILON = 1e-12
NEG_BIG = -1e30


def passed_along(value, axis, steps):
    count = lax.axis_size(axis)
    pairs = [(source, (source + steps) % count) for source in range(count)]
    return lax.ppermute(value, axis, pairs)


def rotate(vectors, positions):
    half_dim = vectors.shape[-1] // 2
    frequency = 10000.0 ** (-2.0 * jnp.arange(half_dim, dtype=jnp.float32) / vectors.shape[-1])
    angles = positions[:, None] * frequency[None, :]
    cosine = jnp.cos(angles)[:, None, :]
    sine_part = jnp.sin(angles)[:, None, :]
    split_pairs = vectors.reshape(vectors.shape[:-1] + (half_dim, 2))
    even_part = split_pairs[..., 0]
    odd_part = split_pairs[..., 1]
    turned = jnp.stack(
        [even_part * cosine - odd_part * sine_part, odd_part * cosine + even_part * sine_part],
        axis=-1,
    )
    return turned.reshape(vectors.shape)


def layer_norm(residual, scale_gain, shift_bias):
    row_mean = jnp.mean(residual, axis=-1, keepdims=True)
    centered = residual - row_mean
    variance = jnp.mean(centered * centered, axis=-1, keepdims=True)
    return centered * lax.rsqrt(variance + EPSILON) * scale_gain + shift_bias


def gelu_exact(upward):
    return jax.nn.gelu(upward, approximate=False)


def run_blocks(step_fn, carry_now, key_piece, first_row, block_keys):
    row_count = key_piece.shape[1]
    width_now = block_keys if row_count % block_keys == 0 else row_count

    def one_turn(index, carry_in):
        begin_at = index * width_now
        sub_piece = lax.dynamic_slice_in_dim(key_piece, begin_at, width_now, 1)
        return step_fn(carry_in, sub_piece, first_row + begin_at)

    return lax.fori_loop(0, row_count // width_now, one_turn, carry_now)


def on_device(
    hidden_in,
    lengths,
    attn_weight,
    attn_bias,
    proj_weight,
    proj_bias,
    first_gain,
    first_shift,
    up_weight,
    up_bias,
    down_weight,
    down_bias,
    second_gain,
    second_shift,
    grad_out,
):
    seq_count, span_rows, model_width = hidden_in.shape
    token_count = seq_count * span_rows
    seq_devices = lax.axis_size("seq")
    my_index = lax.axis_index("seq")
    block_keys = max(span_rows, 512)
    score_scale = HEAD_DIM ** (-0.5)
    offset = my_index * span_rows
    row_index = offset + jnp.arange(span_rows, dtype=jnp.int32)
    positions = row_index.astype(jnp.float32)
    attn_full, attn_bias_full, proj_full, proj_bias_full, gain_one, shift_one = (
        lax.all_gather(attn_weight, ("seq", "batch"), axis=0, tiled=True),
        lax.all_gather(attn_bias, ("seq", "batch"), axis=0, tiled=True),
        lax.all_gather(proj_weight, ("seq", "batch"), axis=0, tiled=True),
        lax.all_gather(proj_bias, ("seq", "batch"), axis=0, tiled=True),
        lax.all_gather(first_gain, ("seq", "batch"), axis=0, tiled=True),
        lax.all_gather(first_shift, ("seq", "batch"), axis=0, tiled=True),
    )
    up_full, up_bias_full, down_full, down_bias_full, gain_two, shift_two = (
        lax.all_gather(up_weight, ("seq", "batch"), axis=0, tiled=True),
        lax.all_gather(up_bias, ("seq", "batch"), axis=0, tiled=True),
        lax.all_gather(down_weight, ("seq", "batch"), axis=0, tiled=True),
        lax.all_gather(down_bias, ("seq", "batch"), axis=0, tiled=True),
        lax.all_gather(second_gain, ("seq", "batch"), axis=0, tiled=True),
        lax.all_gather(second_shift, ("seq", "batch"), axis=0, tiled=True),
    )
    tokens_flat = hidden_in.reshape(token_count, model_width)
    projected = jnp.dot(
        tokens_flat, attn_full, preferred_element_type=jnp.float32
    ) + attn_bias_full.astype(jnp.float32)
    projected = projected.reshape(seq_count, span_rows, 3, HEADS, HEAD_DIM)
    queries = rotate(projected[:, :, 0], positions).astype(jnp.bfloat16)
    keys_low = rotate(projected[:, :, 1], positions).astype(jnp.bfloat16)
    values_low = projected[:, :, 2].astype(jnp.bfloat16)
    key_values = jnp.concatenate(
        [
            keys_low.reshape(seq_count, span_rows, model_width),
            values_low.reshape(seq_count, span_rows, model_width),
        ],
        axis=-1,
    )

    def key_mask(first_row, row_count):
        key_rows = first_row + jnp.arange(row_count, dtype=jnp.int32)
        return (key_rows[None, :] < lengths[:, None])[:, None, None, :]

    def split_pairs(key_piece):
        row_count = key_piece.shape[1]
        keys_part = key_piece[:, :, :model_width].reshape(seq_count, row_count, HEADS, HEAD_DIM)
        values_part = key_piece[:, :, model_width:].reshape(seq_count, row_count, HEADS, HEAD_DIM)
        return (keys_part, values_part)

    def attend_step(carry_in, key_piece, first_row):
        row_max, row_sum, accum = carry_in
        keys_part, values_part = split_pairs(key_piece)
        masked = key_mask(first_row, key_piece.shape[1])
        scores = score_scale * jnp.einsum(
            "sqhd,skhd->shqk", queries, keys_part, preferred_element_type=jnp.float32
        )
        scores = jnp.where(masked, scores, NEG_BIG)
        new_max = jnp.maximum(row_max, jnp.max(scores, axis=-1))
        weights = jnp.where(masked, jnp.exp(scores - new_max[..., None]), 0.0)
        factor = jnp.exp(row_max - new_max)
        row_sum = row_sum * factor + jnp.sum(weights, axis=-1)
        accum = accum * jnp.transpose(factor, (0, 2, 1))[..., None] + jnp.einsum(
            "shqk,skhd->sqhd",
            weights.astype(jnp.bfloat16),
            values_part,
            preferred_element_type=jnp.float32,
        )
        return (new_max, row_sum, accum)

    start_state = (
        jnp.full((seq_count, HEADS, span_rows), NEG_BIG, jnp.float32),
        jnp.zeros((seq_count, HEADS, span_rows), jnp.float32),
        jnp.zeros((seq_count, span_rows, HEADS, HEAD_DIM), jnp.float32),
    )
    row_max, row_sum, accum = run_blocks(
        attend_step,
        start_state,
        lax.all_gather(key_values, "seq", axis=1, tiled=True),
        jnp.int32(0),
        block_keys,
    )
    sum_view = jnp.transpose(row_sum, (0, 2, 1))[..., None]
    attended = accum / sum_view
    attn_rows = attended.reshape(token_count, model_width).astype(jnp.bfloat16)
    mixed = jnp.dot(
        attn_rows, proj_full, preferred_element_type=jnp.float32
    ) + proj_bias_full.astype(jnp.float32)
    normed, norm_back_one = jax.vjp(
        layer_norm,
        tokens_flat.astype(jnp.float32) + mixed,
        gain_one.astype(jnp.float32),
        shift_one.astype(jnp.float32),
    )
    normed_low = normed.astype(jnp.bfloat16)
    upward = jnp.dot(normed_low, up_full, preferred_element_type=jnp.float32) + up_bias_full.astype(
        jnp.float32
    )
    active, gelu_back = jax.vjp(gelu_exact, upward)
    active_low = active.astype(jnp.bfloat16)
    downward = jnp.dot(
        active_low, down_full, preferred_element_type=jnp.float32
    ) + down_bias_full.astype(jnp.float32)
    output_rows, norm_back_two = jax.vjp(
        layer_norm, normed + downward, gain_two.astype(jnp.float32), shift_two.astype(jnp.float32)
    )
    layer_out = output_rows.reshape(seq_count, span_rows, model_width).astype(jnp.bfloat16)
    row_valid = (row_index[None, :] < lengths[:, None]).astype(jnp.float32)
    cotangent = (grad_out.astype(jnp.float32) * row_valid[:, :, None]).reshape(
        token_count, model_width
    )
    d_resid_two, d_gain_two, d_shift_two = norm_back_two(cotangent)
    d_down = d_resid_two.astype(jnp.bfloat16)
    d_down_bias = jnp.sum(d_down.astype(jnp.float32), axis=0)
    d_down_weight = jnp.einsum("tf,td->fd", active_low, d_down, preferred_element_type=jnp.float32)
    d_active = jnp.dot(d_down, down_full.T, preferred_element_type=jnp.float32)
    (d_upward,) = gelu_back(d_active)
    d_up = d_upward.astype(jnp.bfloat16)
    d_up_bias = jnp.sum(d_up.astype(jnp.float32), axis=0)
    d_up_weight = jnp.einsum("td,tf->df", normed_low, d_up, preferred_element_type=jnp.float32)
    d_normed = d_resid_two + jnp.dot(d_up, up_full.T, preferred_element_type=jnp.float32)
    ffn_parts = (
        lax.psum_scatter(d_up_weight, ("seq", "batch"), scatter_dimension=0, tiled=True),
        lax.psum_scatter(d_up_bias, ("seq", "batch"), scatter_dimension=0, tiled=True),
        lax.psum_scatter(d_down_weight, ("seq", "batch"), scatter_dimension=0, tiled=True),
        lax.psum_scatter(d_down_bias, ("seq", "batch"), scatter_dimension=0, tiled=True),
        lax.psum_scatter(d_gain_two, ("seq", "batch"), scatter_dimension=0, tiled=True),
        lax.psum_scatter(d_shift_two, ("seq", "batch"), scatter_dimension=0, tiled=True),
    )
    d_resid_one, d_gain_one, d_shift_one = norm_back_one(d_normed)
    d_mixed = d_resid_one.astype(jnp.bfloat16)
    d_proj_bias = jnp.sum(d_mixed.astype(jnp.float32), axis=0)
    d_proj_weight = jnp.einsum("td,te->de", attn_rows, d_mixed, preferred_element_type=jnp.float32)
    d_attended = jnp.dot(d_mixed, proj_full.T, preferred_element_type=jnp.float32).astype(
        jnp.bfloat16
    )
    d_attended = d_attended.astype(jnp.float32).reshape(seq_count, span_rows, HEADS, HEAD_DIM)
    delta = jnp.transpose(jnp.sum(d_attended * attended, axis=-1), (0, 2, 1))
    delta_scaled = delta / row_sum
    guide = (d_attended / sum_view).astype(jnp.bfloat16)

    def back_step(carry_in, key_piece, first_row):
        d_queries, buffer = carry_in
        keys_part, values_part = split_pairs(key_piece)
        row_count = key_piece.shape[1]
        masked = key_mask(first_row, row_count)
        scores = score_scale * jnp.einsum(
            "sqhd,skhd->shqk", queries, keys_part, preferred_element_type=jnp.float32
        )
        scores = jnp.where(masked, scores, NEG_BIG)
        weights = jnp.where(masked, jnp.exp(scores - row_max[..., None]), 0.0)
        d_weights = jnp.einsum(
            "sqhd,skhd->shqk", guide, values_part, preferred_element_type=jnp.float32
        )
        d_scores = (weights * (d_weights - delta_scaled[..., None])).astype(jnp.bfloat16)
        d_queries = d_queries + score_scale * jnp.einsum(
            "shqk,skhd->sqhd", d_scores, keys_part, preferred_element_type=jnp.float32
        )
        d_keys = score_scale * jnp.einsum(
            "shqk,sqhd->skhd", d_scores, queries, preferred_element_type=jnp.float32
        )
        d_values = jnp.einsum(
            "shqk,sqhd->skhd",
            weights.astype(jnp.bfloat16),
            guide,
            preferred_element_type=jnp.float32,
        )
        new_terms = jnp.concatenate(
            [
                d_keys.reshape(seq_count, row_count, model_width),
                d_values.reshape(seq_count, row_count, model_width),
            ],
            axis=-1,
        )
        current = buffer
        buffer = current + new_terms
        return (d_queries, buffer)

    zero_queries = jnp.zeros((seq_count, span_rows, HEADS, HEAD_DIM), jnp.float32)

    def cycle_turn(turn, carry_in):
        d_queries, pair_piece, grad_piece = carry_in
        owner = (my_index - turn) % seq_devices
        base_row = owner * span_rows

        def owner_step(inner, key_piece, first_row):
            return back_step(inner, key_piece, first_row)

        d_queries, grad_piece = run_blocks(
            owner_step, (d_queries, grad_piece), pair_piece, base_row, block_keys
        )
        grad_piece = passed_along(grad_piece.astype(jnp.bfloat16), "seq", 1).astype(
            grad_piece.dtype
        )
        pair_piece = passed_along(pair_piece, "seq", 1)
        return (d_queries, pair_piece, grad_piece)

    start_cycle = (
        zero_queries,
        key_values,
        jnp.zeros((seq_count, span_rows, 2 * model_width), jnp.float32),
    )
    d_queries, pair_spent, d_pairs = lax.fori_loop(0, seq_devices, cycle_turn, start_cycle)
    d_keys_own = d_pairs[:, :, :model_width].reshape(seq_count, span_rows, HEADS, HEAD_DIM)
    d_values_own = d_pairs[:, :, model_width:].reshape(seq_count, span_rows, HEADS, HEAD_DIM)
    d_projected = jnp.stack(
        [rotate(d_queries, -positions), rotate(d_keys_own, -positions), d_values_own], axis=2
    )
    d_projected = d_projected.reshape(token_count, 3 * model_width).astype(jnp.bfloat16)
    d_attn_bias = jnp.sum(d_projected.astype(jnp.float32), axis=0)
    d_pair_bias = d_attn_bias[: 2 * model_width]
    d_value_bias = d_attn_bias[2 * model_width :]
    d_attn_weight = jnp.einsum(
        "td,tf->df", tokens_flat, d_projected, preferred_element_type=jnp.float32
    )
    grad_hidden = d_resid_one + jnp.dot(
        d_projected, attn_full.T, preferred_element_type=jnp.float32
    )
    attn_parts = (
        lax.psum_scatter(d_attn_weight, ("seq", "batch"), scatter_dimension=0, tiled=True),
        lax.psum_scatter(d_pair_bias, ("seq", "batch"), scatter_dimension=0, tiled=True),
        lax.psum_scatter(d_value_bias, ("seq", "batch"), scatter_dimension=0, tiled=True),
        lax.psum_scatter(d_proj_weight, ("seq", "batch"), scatter_dimension=0, tiled=True),
        lax.psum_scatter(d_proj_bias, ("seq", "batch"), scatter_dimension=0, tiled=True),
        lax.psum_scatter(d_gain_one, ("seq", "batch"), scatter_dimension=0, tiled=True),
        lax.psum_scatter(d_shift_one, ("seq", "batch"), scatter_dimension=0, tiled=True),
    )
    return (
        layer_out,
        grad_hidden.reshape(seq_count, span_rows, model_width),
        attn_parts[0],
        attn_parts[1],
        attn_parts[2],
        attn_parts[3],
        attn_parts[4],
        attn_parts[5],
        attn_parts[6],
        ffn_parts[0],
        ffn_parts[1],
        ffn_parts[2],
        ffn_parts[3],
        ffn_parts[4],
        ffn_parts[5],
    )


def solution(mesh):
    in_specs = (
        P("batch", "seq", None),
        P("batch"),
        P(("seq", "batch"), None),
        P(("seq", "batch")),
        P(("seq", "batch"), None),
        P(("seq", "batch")),
        P(("seq", "batch")),
        P(("seq", "batch")),
        P(("seq", "batch"), None),
        P(("seq", "batch")),
        P(("seq", "batch"), None),
        P(("seq", "batch")),
        P(("seq", "batch")),
        P(("seq", "batch")),
        P("batch", "seq", None),
    )
    out_specs = (
        P("batch", "seq", None),
        P("batch", "seq", None),
        P(("seq", "batch"), None),
        P(("seq", "batch")),
        P(("seq", "batch")),
        P(("seq", "batch"), None),
        P(("seq", "batch")),
        P(("seq", "batch")),
        P(("seq", "batch")),
        P(("seq", "batch"), None),
        P(("seq", "batch")),
        P(("seq", "batch"), None),
        P(("seq", "batch")),
        P(("seq", "batch")),
        P(("seq", "batch")),
    )
    return jax.shard_map(
        on_device, mesh=mesh, in_specs=in_specs, out_specs=out_specs, check_vma=False
    )
```

profile of v0, /device:TPU:0, one launch (start us, length us, event | category | flops | bytes accessed | tf_op | source)
XLA Modules:
  0.0 1025.8 jit_solution(4289925752150631641)
XLA Ops:
  14.7 42.7 %all-reduce.18 = (bf16[3072]{0:T(1024)(128)(2,1)S(1)}, bf16[768]{0:T(1024)(128)(2,1)S(1)}, bf16[2304]{0:T(1024)(128)(2,1)S(1)}, bf16[768]{0:T(1024)(128)(2,1)S(1...) all-reduce(bf16[3072]{0:T(1024)(128)(2,1)S(1)} %dynamic-update-slic, ...), channel_id=1, replica_groups=mesh['seq'=8,'batch'=4] {'seq','batch'}, use_global_device_ids=true, to_apply=%add.4 | all-reduce | flops 9984 | bytes 39936
  58.2 15.5 %all-gather.6.cloned.1.call-done = bf16[768,2304]{1,0:T(8,128)(2,1)} async-done(((bf16[24,2304]{1,0:T(8,128)(2,1)}), bf16[768,2304]{1,0:T(8,128)(2,1)}) %all-gather.6.cloned.1.call-update) | async-done | bytes 3538960 | tf_op jit(solution)/shard_map/all_gather | solution.py:86
  99.4 36.1 %all-gather.8.cloned.1.call-done = bf16[2,1024,1536]{1,2,0:T(8,128)(2,1)} async-done(((bf16[2,128,1536]{1,2,0:T(8,128)(2,1)}), bf16[2,1024,1536]{1,2,0:T(8,128)(2,1)}) %all-gather.8.cloned.1.call-update) | async-done | bytes 6291472 | tf_op jit(solution)/shard_map/all_gather | solution.py:155
  135.5 31.3 %while.50 = (s32[]{:T(128)}, f32[2,12,128]{2,1,0:T(8,128)}, f32[2,12,128]{2,1,0:T(8,128)}, f32[2,128,12,64]{1,3,2,0:T(8,128)}, s32[2]{0:T(128)}, /*index=5*/bf16...) while((s32[]{:T(128)}, f32[2,12,128]{2,1,0:T(8,128)}, ...), condition=%wide.region_3.4_spmd.clone, body=%wide.region_0.3_spmd.clone.sunk | while | flops 423710208 | bytes 55804276 | solution.py:56
  158.6 5.7 fusion.119
  170.4 22.0 %all-gather.10.cloned.1.call-done = bf16[768,768]{1,0:T(8,128)(2,1)} async-done(((bf16[24,768]{1,0:T(8,128)(2,1)}), bf16[768,768]{1,0:T(8,128)(2,1)}) %all-gather.10.cloned.1.call-update) | async-done | bytes 1179664 | tf_op jit(solution)/shard_map/all_gather | solution.py:88
  194.7 63.0 %all-gather.12.cloned.1.call-done = bf16[768,3072]{1,0:T(8,128)(2,1)} async-done(((bf16[24,3072]{1,0:T(8,128)(2,1)}), bf16[768,3072]{1,0:T(8,128)(2,1)}) %all-gather.12.cloned.1.call-update) | async-done | bytes 4718608 | tf_op jit(solution)/shard_map/all_gather | solution.py:94
  257.6 11.8 %multiply_convert_fusion.1 = (bf16[256,3072]{1,0:T(8,128)(2,1)}, f32[256,3072]{1,0:T(8,128)}, f32[256,3072]{1,0:T(8,128)}) fusion(f32[3072]{0:T(1024)S(1)} %copy-done.37, bf16[768,3072]{1,0:T(8,128)(2,1)} %all-gather.12.cloned.1.call-done, f32[256,768]{1,0:T(8,128)S(1)} %get-tuple-element.673, f32[768]{0:T(1024)S(1)} %copy-done.24, f32[768]{0:T(1024)S(1)} %copy-done.21, ...), kind=kOutput, calls=%fused_computation.44 | convolution fusion | flops 1260847104 | bytes 13389824 | tf_op jit(solution)/shard_map/dot_general | solution.py:172
  269.5 53.2 %all-gather.14.cloned.1.call-done = bf16[3072,768]{1,0:T(8,128)(2,1)} async-done(((bf16[96,768]{1,0:T(8,128)(2,1)}), bf16[3072,768]{1,0:T(8,128)(2,1)}) %all-gather.14.cloned.1.call-update) | async-done | bytes 4718608 | tf_op jit(solution)/shard_map/all_gather | solution.py:96
  345.5 234.4 %while.51 = (s32[]{:T(128)}, f32[2,128,12,64]{1,3,2,0:T(8,128)}, bf16[2,128,1536]{1,2,0:T(8,128)(2,1)}, f32[2,128,1536]{1,2,0:T(8,128)S(1)}, s32[]{:T(128)}, /*i...) while((s32[]{:T(128)}, f32[2,128,12,64]{1,3,2,0:T(8,128)}, ...), condition=%wide.region_14.15_spmd.clone, body=%wide.region_13.14_spmd.clone.sunk | while | flops 257556880 | bytes 30353328 | solution.py:279
  357.7 8.6 collective-permute-done.1
  367.5 7.2 collective-permute-done
  385.6 9.2 collective-permute-done.1
  396.1 11.4 %collective-permute-done = bf16[2,128,1536]{1,2,0:T(8,128)(2,1)} collective-permute-done((bf16[2,128,1536]{1,2,0:T(8,128)(2,1)S(1)}, bf16[2,128,1536]{1,2,0:T(8,128)(2,1)}, u32[]{:S(2)}, u32[]{:S(2)}) %collective-permute-start) | collective-permute-done | bytes 786464 | tf_op jit(solution)/shard_map/while/body/eval_jaxpr/ppermute | solution.py:17
  417.9 10.1 collective-permute-done.1
  429.2 7.2 collective-permute-done
  446.7 10.4 %collective-permute-done.1 = bf16[2,128,1536]{1,2,0:T(8,128)(2,1)} collective-permute-done((bf16[2,128,1536]{1,2,0:T(8,128)(2,1)}, bf16[2,128,1536]{1,2,0:T(8,128)(2,1)}, u32[]{:S(2)}, u32[]{:S(2)}) %collective-permute-start.1) | collective-permute-done | bytes 786464 | tf_op jit(solution)/shard_map/while/body/eval_jaxpr/ppermute | solution.py:17
  458.3 7.2 collective-permute-done
  475.8 9.8 collective-permute-done.1
  486.9 7.2 collective-permute-done
  504.4 9.8 collective-permute-done.1
  515.5 7.2 collective-permute-done
  533.0 9.8 collective-permute-done.1
  544.1 7.2 collective-permute-done
  561.6 9.8 collective-permute-done.1
  572.7 7.2 collective-permute-done
  586.7 17.9 %convert_reduce_fusion.1 = (f32[3,12,64]{2,1,0:T(8,128)}, bf16[2,128,3,12,64]{1,0,4,3,2:T(2,128)(2,1)S(1)}) fusion(bf16[2,128,1,12,64]{1,0,4,3,2:T(2,128)(2,1)S(1)} %copy.65, bf16[2,128,1,12,64]{1,0,4,3,2:T(2,128)(2,1)S(1)} %bitcast.184, bf16[2,128,1,12,64]{1,0,4,3,2:T(2,128)(2,1)S(1)} %bitcast.182), kind=kLoop, calls=%fused_computation.59 | loop fusion | flops 2356992 | bytes 2368512 | tf_op jit(solution)/shard_map/reduce_sum | solution.py:286
  608.6 8.1 copy.68
  631.1 40.5 %all-reduce.17 = (f32[1536]{0:T(1024)S(1)}, f32[768]{0:T(1024)S(1)}, f32[768]{0:T(1024)S(1)}, f32[768]{0:T(1024)S(1)}, f32[768]{0:T(1024)S(1)}, /*index=5*/f32[3...) all-reduce(f32[1536]{0:T(1024)S(1)} %slice.102, ...), channel_id=3, replica_groups=mesh['seq'=8,'batch'=4] {'seq','batch'}, use_global_device_ids=true, to_apply=%region_17.18.clone | all-reduce | flops 9984 | bytes 79872
  680.9 54.6 %reduce-scatter.13.cloned.1.call-done = f32[24,2304]{1,0:T(8,128)} async-done(((f32[768,2304]{1,0:T(8,128)}), f32[24,2304]{1,0:T(8,128)}) %reduce-scatter.13.cloned.1.call-update) | async-done | bytes 221200
  735.5 141.3 %reduce-scatter.9.cloned.1.call-done = f32[24,3072]{1,0:T(8,128)} async-done(((f32[768,3072]{1,0:T(8,128)}), f32[24,3072]{1,0:T(8,128)}) %reduce-scatter.9.cloned.1.call-update) | async-done | bytes 294928 | tf_op jit(solution)/shard_map/reduce_scatter | solution.py:199
  876.7 142.3 %reduce-scatter.11.cloned.1.call-done = f32[96,768]{1,0:T(8,128)} async-done(((f32[3072,768]{1,0:T(8,128)}), f32[96,768]{1,0:T(8,128)}) %reduce-scatter.11.cloned.1.call-update) | async-done | bytes 294928 | tf_op jit(solution)/shard_map/reduce_scatter | solution.py:201
  (383 shorter events, 216.1 us)
Async XLA Ops:
  7.2 66.6 %all-gather.6.cloned.1.call-start = ((), (), s32[]{:S(2)}) async-start(), calls=%async_computation.4 | async-start | bytes 3649536 | tf_op jit(solution)/shard_map/all_gather | solution.py:86
  7.9 127.6 %all-gather.8.cloned.1.call-start = ((), (), s32[]{:S(2)}) async-start(), calls=%async_computation.5 | async-start | bytes 7077888 | tf_op jit(solution)/shard_map/all_gather | solution.py:155
  89.9 102.6 %all-gather.10.cloned.1.call-start = ((), (), s32[]{:S(2)}) async-start(), calls=%async_computation.6 | async-start | bytes 1216512 | tf_op jit(solution)/shard_map/all_gather | solution.py:88
  90.6 167.0 %all-gather.12.cloned.1.call-start = ((), (), s32[]{:S(2)}) async-start(), calls=%async_computation.7 | async-start | bytes 4866048 | tf_op jit(solution)/shard_map/all_gather | solution.py:94
  91.2 231.5 %all-gather.14.cloned.1.call-start = ((), (), s32[]{:S(2)}) async-start(), calls=%async_computation.8 | async-start | bytes 4866048 | tf_op jit(solution)/shard_map/all_gather | solution.py:96
  91.8 589.1 %reduce-scatter.7.cloned.1.call-start = ((), (), s32[]{:S(2)}) async-start(), calls=%async_computation.9 | async-start | bytes 2433024 | tf_op jit(solution)/shard_map/reduce_scatter | solution.py:299
  166.8 90.9 %copy-start.21 = (f32[768]{0:T(1024)S(1)}, f32[768]{0:T(1024)}, u32[]{:S(2)}) copy-start(f32[768]{0:T(1024)} %convert_element_type.180) | copy-start | bytes 9220
  166.8 90.9 %copy-start.24 = (f32[768]{0:T(1024)S(1)}, f32[768]{0:T(1024)}, u32[]{:S(2)}) copy-start(f32[768]{0:T(1024)} %convert_element_type.181) | copy-start | bytes 9220
  166.8 90.9 %copy-start.37 = (f32[3072]{0:T(1024)S(1)}, f32[3072]{0:T(1024)}, u32[]{:S(2)}) copy-start(f32[3072]{0:T(1024)} %convert_element_type.183) | copy-start | bytes 36868
  194.4 140.9 %copy-start.3 = (f32[256,768]{1,0:T(8,128)}, f32[256,768]{1,0:T(8,128)S(1)}, u32[]{:S(2)}) copy-start(f32[256,768]{1,0:T(8,128)S(1)} %get-tuple-element.673) | copy-start | bytes 2359300
  194.4 140.8 %copy-start.28 = (f32[256]{0:T(256)}, f32[256]{0:T(256)S(1)}, u32[]{:S(2)}) copy-start(f32[256]{0:T(256)S(1)} %broadcast_multiply_fusion.1) | copy-start | bytes 3076
  194.7 140.6 %copy-start.35 = (f32[256]{0:T(256)}, f32[256]{0:T(256)S(1)}, u32[]{:S(2)}) copy-start(f32[256]{0:T(256)S(1)} %fusion.45) | copy-start | bytes 3076
  194.7 128.0 %copy-start.41 = (f32[768]{0:T(1024)S(1)}, f32[768]{0:T(1024)}, u32[]{:S(2)}) copy-start(f32[768]{0:T(1024)} %convert_element_type.185) | copy-start | bytes 9220
  345.5 390.0 %reduce-scatter.13.cloned.1.call-start = ((), (), s32[]{:S(2)}) async-start(), calls=%async_computation.12 | async-start | bytes 7299072
  353.6 12.6 %collective-permute-start.1 = (bf16[2,128,1536]{1,2,0:T(8,128)(2,1)}, bf16[2,128,1536]{1,2,0:T(8,128)(2,1)}, u32[]{:S(2)}, u32[]{:S(2)}) collective-permute-start(bf16[2,128,1536]{1,2,0:T(8,128)(2,1)} %fusion.133), channel_id=1, source_target_pairs={{0,4},{4,8},{8,12},{12,16},{16,20},{20,24},{24,28},{28,0},{1,5},{5... | collective-permute-start | bytes 2359304 | tf_op jit(solution)/shard_map/while/body/eval_jaxpr/ppermute | solution.py:17
  353.9 20.8 %collective-permute-start = (bf16[2,128,1536]{1,2,0:T(8,128)(2,1)S(1)}, bf16[2,128,1536]{1,2,0:T(8,128)(2,1)}, u32[]{:S(2)}, u32[]{:S(2)}) collective-permute-start(bf16[2,128,1536]{1,2,0:T(8,128)(2,1)S(1)} %copy.119), channel_id=1, source_target_pairs={{0,4},{4,8},{8,12},{12,16},{16,20},{20,24},{24,28},{28,0},{1,5},{5... | collective-permute-start | bytes 2359304 | tf_op jit(solution)/shard_map/while/body/eval_jaxpr/ppermute | solution.py:17
  382.2 12.6 %collective-permute-start.1 = (bf16[2,128,1536]{1,2,0:T(8,128)(2,1)}, bf16[2,128,1536]{1,2,0:T(8,128)(2,1)}, u32[]{:S(2)}, u32[]{:S(2)}) collective-permute-start(bf16[2,128,1536]{1,2,0:T(8,128)(2,1)} %fusion.133), channel_id=1, source_target_pairs={{0,4},{4,8},{8,12},{12,16},{16,20},{20,24},{24,28},{28,0},{1,5},{5... | collective-permute-start | bytes 2359304 | tf_op jit(solution)/shard_map/while/body/eval_jaxpr/ppermute | solution.py:17
  382.2 25.3 %collective-permute-start = (bf16[2,128,1536]{1,2,0:T(8,128)(2,1)S(1)}, bf16[2,128,1536]{1,2,0:T(8,128)(2,1)}, u32[]{:S(2)}, u32[]{:S(2)}) collective-permute-start(bf16[2,128,1536]{1,2,0:T(8,128)(2,1)S(1)} %copy.119), channel_id=1, source_target_pairs={{0,4},{4,8},{8,12},{12,16},{16,20},{20,24},{24,28},{28,0},{1,5},{5... | collective-permute-start | bytes 2359304 | tf_op jit(solution)/shard_map/while/body/eval_jaxpr/ppermute | solution.py:17
  415.1 12.9 %collective-permute-start.1 = (bf16[2,128,1536]{1,2,0:T(8,128)(2,1)}, bf16[2,128,1536]{1,2,0:T(8,128)(2,1)}, u32[]{:S(2)}, u32[]{:S(2)}) collective-permute-start(bf16[2,128,1536]{1,2,0:T(8,128)(2,1)} %fusion.133), channel_id=1, source_target_pairs={{0,4},{4,8},{8,12},{12,16},{16,20},{20,24},{24,28},{28,0},{1,5},{5... | collective-permute-start | bytes 2359304 | tf_op jit(solution)/shard_map/while/body/eval_jaxpr/ppermute | solution.py:17
  415.1 21.3 %collective-permute-start = (bf16[2,128,1536]{1,2,0:T(8,128)(2,1)S(1)}, bf16[2,128,1536]{1,2,0:T(8,128)(2,1)}, u32[]{:S(2)}, u32[]{:S(2)}) collective-permute-start(bf16[2,128,1536]{1,2,0:T(8,128)(2,1)S(1)} %copy.119), channel_id=1, source_target_pairs={{0,4},{4,8},{8,12},{12,16},{16,20},{20,24},{24,28},{28,0},{1,5},{5... | collective-permute-start | bytes 2359304 | tf_op jit(solution)/shard_map/while/body/eval_jaxpr/ppermute | solution.py:17
  443.9 13.2 %collective-permute-start.1 = (bf16[2,128,1536]{1,2,0:T(8,128)(2,1)}, bf16[2,128,1536]{1,2,0:T(8,128)(2,1)}, u32[]{:S(2)}, u32[]{:S(2)}) collective-permute-start(bf16[2,128,1536]{1,2,0:T(8,128)(2,1)} %fusion.133), channel_id=1, source_target_pairs={{0,4},{4,8},{8,12},{12,16},{16,20},{20,24},{24,28},{28,0},{1,5},{5... | collective-permute-start | bytes 2359304 | tf_op jit(solution)/shard_map/while/body/eval_jaxpr/ppermute | solution.py:17
  443.9 21.6 %collective-permute-start = (bf16[2,128,1536]{1,2,0:T(8,128)(2,1)S(1)}, bf16[2,128,1536]{1,2,0:T(8,128)(2,1)}, u32[]{:S(2)}, u32[]{:S(2)}) collective-permute-start(bf16[2,128,1536]{1,2,0:T(8,128)(2,1)S(1)} %copy.119), channel_id=1, source_target_pairs={{0,4},{4,8},{8,12},{12,16},{16,20},{20,24},{24,28},{28,0},{1,5},{5... | collective-permute-start | bytes 2359304 | tf_op jit(solution)/shard_map/while/body/eval_jaxpr/ppermute | solution.py:17
  473.1 12.6 %collective-permute-start.1 = (bf16[2,128,1536]{1,2,0:T(8,128)(2,1)}, bf16[2,128,1536]{1,2,0:T(8,128)(2,1)}, u32[]{:S(2)}, u32[]{:S(2)}) collective-permute-start(bf16[2,128,1536]{1,2,0:T(8,128)(2,1)} %fusion.133), channel_id=1, source_target_pairs={{0,4},{4,8},{8,12},{12,16},{16,20},{20,24},{24,28},{28,0},{1,5},{5... | collective-permute-start | bytes 2359304 | tf_op jit(solution)/shard_map/while/body/eval_jaxpr/ppermute | solution.py:17
  473.1 21.1 %collective-permute-start = (bf16[2,128,1536]{1,2,0:T(8,128)(2,1)S(1)}, bf16[2,128,1536]{1,2,0:T(8,128)(2,1)}, u32[]{:S(2)}, u32[]{:S(2)}) collective-permute-start(bf16[2,128,1536]{1,2,0:T(8,128)(2,1)S(1)} %copy.119), channel_id=1, source_target_pairs={{0,4},{4,8},{8,12},{12,16},{16,20},{20,24},{24,28},{28,0},{1,5},{5... | collective-permute-start | bytes 2359304 | tf_op jit(solution)/shard_map/while/body/eval_jaxpr/ppermute | solution.py:17
  501.7 12.6 %collective-permute-start.1 = (bf16[2,128,1536]{1,2,0:T(8,128)(2,1)}, bf16[2,128,1536]{1,2,0:T(8,128)(2,1)}, u32[]{:S(2)}, u32[]{:S(2)}) collective-permute-start(bf16[2,128,1536]{1,2,0:T(8,128)(2,1)} %fusion.133), channel_id=1, source_target_pairs={{0,4},{4,8},{8,12},{12,16},{16,20},{20,24},{24,28},{28,0},{1,5},{5... | collective-permute-start | bytes 2359304 | tf_op jit(solution)/shard_map/while/body/eval_jaxpr/ppermute | solution.py:17
  501.7 21.1 %collective-permute-start = (bf16[2,128,1536]{1,2,0:T(8,128)(2,1)S(1)}, bf16[2,128,1536]{1,2,0:T(8,128)(2,1)}, u32[]{:S(2)}, u32[]{:S(2)}) collective-permute-start(bf16[2,128,1536]{1,2,0:T(8,128)(2,1)S(1)} %copy.119), channel_id=1, source_target_pairs={{0,4},{4,8},{8,12},{12,16},{16,20},{20,24},{24,28},{28,0},{1,5},{5... | collective-permute-start | bytes 2359304 | tf_op jit(solution)/shard_map/while/body/eval_jaxpr/ppermute | solution.py:17
  530.3 12.6 %collective-permute-start.1 = (bf16[2,128,1536]{1,2,0:T(8,128)(2,1)}, bf16[2,128,1536]{1,2,0:T(8,128)(2,1)}, u32[]{:S(2)}, u32[]{:S(2)}) collective-permute-start(bf16[2,128,1536]{1,2,0:T(8,128)(2,1)} %fusion.133), channel_id=1, source_target_pairs={{0,4},{4,8},{8,12},{12,16},{16,20},{20,24},{24,28},{28,0},{1,5},{5... | collective-permute-start | bytes 2359304 | tf_op jit(solution)/shard_map/while/body/eval_jaxpr/ppermute | solution.py:17
  530.3 21.1 %collective-permute-start = (bf16[2,128,1536]{1,2,0:T(8,128)(2,1)S(1)}, bf16[2,128,1536]{1,2,0:T(8,128)(2,1)}, u32[]{:S(2)}, u32[]{:S(2)}) collective-permute-start(bf16[2,128,1536]{1,2,0:T(8,128)(2,1)S(1)} %copy.119), channel_id=1, source_target_pairs={{0,4},{4,8},{8,12},{12,16},{16,20},{20,24},{24,28},{28,0},{1,5},{5... | collective-permute-start | bytes 2359304 | tf_op jit(solution)/shard_map/while/body/eval_jaxpr/ppermute | solution.py:17
  558.8 12.6 %collective-permute-start.1 = (bf16[2,128,1536]{1,2,0:T(8,128)(2,1)}, bf16[2,128,1536]{1,2,0:T(8,128)(2,1)}, u32[]{:S(2)}, u32[]{:S(2)}) collective-permute-start(bf16[2,128,1536]{1,2,0:T(8,128)(2,1)} %fusion.133), channel_id=1, source_target_pairs={{0,4},{4,8},{8,12},{12,16},{16,20},{20,24},{24,28},{28,0},{1,5},{5... | collective-permute-start | bytes 2359304 | tf_op jit(solution)/shard_map/while/body/eval_jaxpr/ppermute | solution.py:17
  558.9 21.1 %collective-permute-start = (bf16[2,128,1536]{1,2,0:T(8,128)(2,1)S(1)}, bf16[2,128,1536]{1,2,0:T(8,128)(2,1)}, u32[]{:S(2)}, u32[]{:S(2)}) collective-permute-start(bf16[2,128,1536]{1,2,0:T(8,128)(2,1)S(1)} %copy.119), channel_id=1, source_target_pairs={{0,4},{4,8},{8,12},{12,16},{16,20},{20,24},{24,28},{28,0},{1,5},{5... | collective-permute-start | bytes 2359304 | tf_op jit(solution)/shard_map/while/body/eval_jaxpr/ppermute | solution.py:17
  616.7 260.0 %reduce-scatter.9.cloned.1.call-start = ((), (), s32[]{:S(2)}) async-start(), calls=%async_computation.10 | async-start | bytes 9732096 | tf_op jit(solution)/shard_map/reduce_scatter | solution.py:199
  623.6 395.5 %reduce-scatter.11.cloned.1.call-start = ((), (), s32[]{:S(2)}) async-start(), calls=%async_computation.11 | async-start | bytes 9732096 | tf_op jit(solution)/shard_map/reduce_scatter | solution.py:201
  (63 other events, 309.7 us)
Sparse Core Ops, SparseCore 0:
  10.8 62.9 all-gather.5
  90.0 45.4 all-gather.7
  138.3 54.0 all-gather.9
  195.1 62.4 all-gather.11
  260.3 62.3 all-gather.13
  345.6 117.0 reduce-scatter.6
  616.8 118.5 reduce-scatter.12
  741.9 134.7 reduce-scatter.8
  884.2 134.7 reduce-scatter.10
where the time goes:
time: 1030 us
  waiting for transfers between devices  670 us (65%)
  matrix products  126 us (12%)
  blocking collectives  83.2 us (8%)
  other arithmetic  76.4 us (7%)
  local copies, waits for them, and re-layouts  51.9 us (5%)
  between operations  14.7 us (1%)
    reduce_scatter x1, waiting for transfers between devices, on_device(): lax.psum_scatter(d_down_weight, ('seq', 'batch'), scatter_dimension=0, ti...  142 us
    reduce_scatter x1, waiting for transfers between devices, on_device(): lax.psum_scatter(d_up_weight, ('seq', 'batch'), scatter_dimension=0, tile...  141 us
    ppermute x16, waiting for transfers between devices, passed_along(): return lax.ppermute(value, axis, pairs)  139 us
    unnamed x2, blocking collectives  83.2 us
    all_gather x1, waiting for transfers between devices, on_device(): lax.all_gather(up_weight, ('seq', 'batch'), axis=0, tiled=True)  63 us
    unnamed x10, waiting for transfers between devices  57.1 us
    all_gather x1, waiting for transfers between devices, on_device(): lax.all_gather(down_weight, ('seq', 'batch'), axis=0, tiled=True)  53.2 us
    all_gather x1, waiting for transfers between devices, on_device(): lax.all_gather(key_values, 'seq', axis=1, tiled=True)  36.1 us
  transfers between devices with their start and end apart: 25, of which 24 were waited for; matrix products, arithmetic and copies ran while one was open for 21% of the time, Pallas kernels for 0%

commit v1 on v0

--- a/solution.py
+++ b/solution.py
@@ -320,6 +320,356 @@
     )
 
 
+SEQ_SIDE = 8
+BATCH_SIDE = 4
+GROUP = 192
+EVEN = (0, 2, 4, 6)
+ODD = (1, 3, 5, 7)
+
+
+def swap_seq(value, mask):
+    return lax.ppermute(value, "seq", [(i, i ^ mask) for i in range(SEQ_SIDE)])
+
+
+def swap_batch(value, mask):
+    return lax.ppermute(value, "batch", [(i, i ^ mask) for i in range(BATCH_SIDE)])
+
+
+def in_order(bit, mine, other, axis):
+    low = jnp.where(bit == 0, mine, other)
+    high = jnp.where(bit == 0, other, mine)
+    return jnp.stack([low, high], axis=axis)
+
+
+def pick(value, index, axis=0):
+    return lax.dynamic_index_in_dim(value, index, axis, keepdims=False)
+
+
+def turn(vectors, cosine, sine):
+    left = jnp.roll(vectors, -1, axis=-1)
+    right = jnp.roll(vectors, 1, axis=-1)
+    even = (jnp.arange(vectors.shape[-1]) % 2) == 0
+    return vectors * cosine + jnp.where(even, left, right) * sine
+
+
+def gather_up(piece, x, y, z):
+    far = [swap_batch(piece, k) for k in (1, 2, 3)]
+    stacked = jnp.stack([piece] + far, axis=0)
+    column = jnp.stack([pick(stacked, k ^ z) for k in range(4)], axis=1)
+    n = piece.shape[-1]
+    column = column.reshape(2, 96, n)
+    first, second = column[0], column[1]
+    first = in_order(x, first, swap_seq(first, 2), 0)
+    second = in_order(y, second, swap_seq(second, 4), 0)
+    first = in_order(y, first, swap_seq(first, 4), 0)
+    second = in_order(x, second, swap_seq(second, 2), 1)
+    return jnp.stack([first, second], axis=2).reshape(768, n)
+
+
+def gather_down(piece, x, y, z):
+    far = [swap_batch(piece, k) for k in (1, 2, 3)]
+    stacked = jnp.stack([piece] + far, axis=0)
+    column = jnp.stack([pick(stacked, k ^ z) for k in range(4)], axis=0)
+    n = piece.shape[-1]
+    first, second = column[:2], column[2:]
+    first = in_order(x, first, swap_seq(first, 2), 0)
+    second = in_order(y, second, swap_seq(second, 4), 0)
+    first = in_order(y, first, swap_seq(first, 4), 0)
+    second = in_order(x, second, swap_seq(second, 2), 1)
+    return jnp.concatenate([first, second], axis=2).reshape(1536, n)
+
+
+def add_low(left, right):
+    return (left.astype(jnp.float32) + right.astype(jnp.float32)).astype(jnp.bfloat16)
+
+
+def halve(value, bit, mask, axis):
+    return add_low(pick(value, bit, axis), swap_seq(pick(value, 1 - bit, axis), mask))
+
+
+def scatter_last(value, z):
+    total = pick(value, z).astype(jnp.float32)
+    for k in (1, 2, 3):
+        total = total + swap_batch(pick(value, z ^ k), k).astype(jnp.float32)
+    return total
+
+
+def scatter_up(value, x, y, z):
+    n = value.shape[-1]
+    value = value.reshape(2, 2, 2, 96, n)
+    first, second = value[:, :, 0], value[:, :, 1]
+    first = halve(halve(first, y, 4, 0), x, 2, 0)
+    second = halve(halve(second, x, 2, 1), y, 4, 0)
+    both = jnp.stack([first, second], axis=0).reshape(2, 4, 24, n)
+    return scatter_last(jnp.transpose(both, (1, 0, 2, 3)), z)
+
+
+def scatter_down(value, x, y, z):
+    n = value.shape[-1]
+    value = value.reshape(2, 2, 4, 96, n)
+    first, second = value[:, :, :2], value[:, :, 2:]
+    first = halve(halve(first, y, 4, 0), x, 2, 0)
+    second = halve(halve(second, x, 2, 1), y, 4, 0)
+    return scatter_last(jnp.concatenate([first, second], axis=0), z)
+
+
+def split_layer(
+    hidden_in,
+    lengths,
+    attn_weight,
+    attn_bias,
+    proj_weight,
+    proj_bias,
+    first_gain,
+    first_shift,
+    up_weight,
+    up_bias,
+    down_weight,
+    down_bias,
+    second_gain,
+    second_shift,
+    grad_out,
+):
+    both_axes = ("seq", "batch")
+    f32, bf16 = jnp.float32, jnp.bfloat16
+    _, span_rows, width = hidden_in.shape
+    hidden_units = up_weight.shape[1]
+    rows_all = SEQ_SIDE * span_rows
+    s = lax.axis_index("seq")
+    z = lax.axis_index("batch")
+    core, x, y = s & 1, (s >> 1) & 1, s >> 2
+    group = s & 3
+    scale = HEAD_DIM ** (-0.5)
+    heads_here = GROUP // HEAD_DIM
+
+    small = jnp.concatenate(
+        [attn_bias, proj_bias, first_gain, first_shift, down_bias, second_gain, second_shift, up_bias]
+    )
+    small_all = lax.all_gather(small[None], both_axes, axis=0, tiled=True).astype(f32)
+    attn_bias_all = small_all[:, :72].reshape(3, 4, GROUP)
+    vectors = [small_all[:, 72 + 24 * i : 96 + 24 * i].reshape(width) for i in range(6)]
+    proj_bias_all, gain_one, shift_one, down_bias_all, gain_two, shift_two = vectors
+    up_bias_all = small_all[:, 216:].reshape(4, 2, 384)
+    up_bias_here = pick(up_bias_all, core, 1).reshape(1536)
+    bias_here = pick(attn_bias_all, group, 1).reshape(3 * GROUP)
+
+    by_group = attn_weight.reshape(24, 3, 4, GROUP).transpose(2, 0, 1, 3).reshape(4, 24, 3 * GROUP)
+    sent = jnp.broadcast_to(by_group[None, :, None], (2, 4, 4, 24, 3 * GROUP)).reshape(
+        32, 24, 3 * GROUP
+    )
+    weight_here = lax.all_to_all(sent, both_axes, 0, 0, tiled=True).reshape(width, 3 * GROUP)
+
+    mine = pick(hidden_in, y)
+    other = pick(hidden_in, 1 - y)
+    even_rows = jnp.concatenate([mine, swap_seq(mine, 2), swap_seq(other, 4), swap_seq(other, 6)])
+    rows_here = jnp.concatenate([even_rows, swap_seq(even_rows, 1)])
+    block_owner = jnp.array([s ^ j for j in EVEN + ODD])
+    positions = (block_owner[:, None] * span_rows + jnp.arange(span_rows)[None, :]).reshape(-1)
+    length = pick(lengths, y)
+
+    up_view = up_weight.reshape(24, 4, 2, 384)
+    proj_view = proj_weight.reshape(24, 2, 384)
+
+    def half_rows(which):
+        return jnp.concatenate(
+            [pick(up_view, which, 2).reshape(24, 1536), pick(proj_view, which, 1)], axis=-1
+        )
+
+    chip_rows = in_order(core, half_rows(core), swap_seq(half_rows(1 - core), 1), 0)
+    up_proj = gather_up(chip_rows, x, y, z)
+    up_here = up_proj[:, :1536]
+    proj_half = up_proj[:, 1536:]
+    proj_all = in_order(core, proj_half, swap_seq(proj_half, 1), 1).reshape(width, width)
+    down_here = gather_down(down_weight, x, y, z)
+
+    projected = jnp.dot(rows_here, weight_here, preferred_element_type=f32) + bias_here
+    frequency = 10000.0 ** (-2.0 * (jnp.arange(HEAD_DIM) // 2).astype(f32) / HEAD_DIM)
+    angles = positions.astype(f32)[:, None] * frequency[None, :]
+    cosine = jnp.tile(jnp.cos(angles), (1, heads_here))
+    sine = jnp.tile(
+        jnp.sin(angles) * jnp.where(jnp.arange(HEAD_DIM) % 2 == 0, -1.0, 1.0), (1, heads_here)
+    )
+
+    def by_head(value):
+        return value.reshape(rows_all, heads_here, HEAD_DIM).transpose(1, 0, 2)
+
+    def merged(value):
+        return value.transpose(1, 0, 2).reshape(rows_all, GROUP)
+
+    queries = by_head(turn(projected[:, :GROUP], cosine, sine).astype(bf16))
+    keys = by_head(turn(projected[:, GROUP : 2 * GROUP], cosine, sine).astype(bf16))
+    values = by_head(projected[:, 2 * GROUP :].astype(bf16))
+    valid = (positions < length)[None, None, :]
+    scores = scale * jnp.einsum("hqd,hkd->hqk", queries, keys, preferred_element_type=f32)
+    scores = jnp.where(valid, scores, NEG_BIG)
+    row_max = jnp.max(scores, axis=-1, keepdims=True)
+    weights = jnp.where(valid, jnp.exp(scores - row_max), 0.0)
+    row_sum = jnp.sum(weights, axis=-1, keepdims=True)
+    weights_low = weights.astype(bf16)
+    attended = (
+        jnp.einsum("hqk,hkd->hqd", weights_low, values, preferred_element_type=f32) / row_sum
+    )
+
+    sent = merged(attended).astype(bf16).reshape(8, span_rows, GROUP)
+    came = swap_seq(sent[4:], 1)
+    pair = jnp.concatenate(
+        [jnp.where(core == 0, sent[:4], came), jnp.where(core == 0, came, sent[:4])], axis=-1
+    )
+
+    def columns(mine_part, other_part):
+        return jnp.concatenate(
+            [
+                jnp.where(x == 0, mine_part, other_part),
+                jnp.where(x == 0, other_part, mine_part),
+            ],
+            axis=-1,
+        )
+
+    attn_rows = jnp.concatenate(
+        [
+            columns(pair[0], swap_seq(pair[1], 2)),
+            columns(swap_seq(pair[2], 4), swap_seq(pair[3], 6)),
+        ],
+        axis=0,
+    )
+    tokens = jnp.concatenate([mine, other], axis=0)
+
+    mixed = jnp.dot(attn_rows, proj_all, preferred_element_type=f32) + proj_bias_all
+    normed, norm_back_one = jax.vjp(layer_norm, tokens.astype(f32) + mixed, gain_one, shift_one)
+    normed_mine = normed.astype(bf16)
+    normed_low = jnp.concatenate([normed_mine, swap_seq(normed_mine, 1)], axis=0)
+    upward = jnp.dot(normed_low, up_here, preferred_element_type=f32) + up_bias_here
+    active, gelu_back = jax.vjp(gelu_exact, upward)
+    active_low = active.astype(bf16)
+    part = jnp.dot(active_low, down_here, preferred_element_type=f32)
+    downward = part[:256] + swap_seq(part[256:].astype(bf16), 1).astype(f32) + down_bias_all
+    output_rows, norm_back_two = jax.vjp(layer_norm, normed + downward, gain_two, shift_two)
+
+    row_index = s * span_rows + jnp.arange(span_rows, dtype=jnp.int32)
+
+    def by_sequence(value, dtype):
+        value = value.reshape(2, span_rows, width)
+        return jnp.where(y == 0, value, value[::-1]).astype(dtype)
+
+    layer_out = by_sequence(output_rows, bf16)
+    lengths_here = jnp.stack([length, pick(lengths, 1 - y)])
+    row_valid = (row_index[None, :] < lengths_here[:, None]).astype(f32).reshape(-1, 1)
+    cotangent = (
+        jnp.concatenate([pick(grad_out, y), pick(grad_out, 1 - y)], axis=0).astype(f32) * row_valid
+    )
+    d_resid_two, d_gain_two, d_shift_two = norm_back_two(cotangent)
+    d_down_mine = d_resid_two.astype(bf16)
+    d_down_bias = jnp.sum(d_down_mine.astype(f32), axis=0)
+    d_down = jnp.concatenate([d_down_mine, swap_seq(d_down_mine, 1)], axis=0)
+    d_down_weight = jnp.einsum("tf,td->fd", active_low, d_down, preferred_element_type=f32)
+    grad_down_weight = scatter_down(d_down_weight.astype(bf16), x, y, z)
+    d_active = jnp.dot(d_down, down_here.T, preferred_element_type=f32)
+    (d_upward,) = gelu_back(d_active)
+    d_up = d_upward.astype(bf16)
+    d_up_bias = jnp.sum(d_up.astype(f32), axis=0)
+    d_up_weight = jnp.einsum("td,tf->df", normed_low, d_up, preferred_element_type=f32)
+    part = jnp.dot(d_up, up_here.T, preferred_element_type=f32)
+    d_normed = d_resid_two + part[:256] + swap_seq(part[256:].astype(bf16), 1).astype(f32)
+    d_resid_one, d_gain_one, d_shift_one = norm_back_one(d_normed)
+    d_mixed = d_resid_one.astype(bf16)
+    d_proj_bias = jnp.sum(d_mixed.astype(f32), axis=0)
+    d_proj_weight = jnp.einsum("td,te->de", attn_rows, d_mixed, preferred_element_type=f32)
+    d_attended = jnp.dot(d_mixed, proj_all.T, preferred_element_type=f32).astype(bf16)
+
+    d_proj_view = d_proj_weight.astype(bf16).reshape(width, 2, 384)
+    d_proj_half = halve(d_proj_view, core, 1, 1)
+    d_up_proj = jnp.concatenate([d_up_weight.astype(bf16), d_proj_half], axis=-1)
+    d_chip_rows = scatter_up(d_up_proj, x, y, z)
+    d_sent = pick(d_chip_rows, 1 - core).astype(bf16)
+    d_came = swap_seq(d_sent, 1).astype(f32)
+    d_own = pick(d_chip_rows, core)
+    low_half = jnp.where(core == 0, d_own, d_came)
+    high_half = jnp.where(core == 0, d_came, d_own)
+    grad_up_weight = jnp.stack(
+        [low_half[:, :1536].reshape(24, 4, 384), high_half[:, :1536].reshape(24, 4, 384)], axis=2
+    ).reshape(24, hidden_units)
+    grad_proj_weight = jnp.concatenate([low_half[:, 1536:], high_half[:, 1536:]], axis=-1)
+
+    d_view = d_attended.reshape(2, span_rows, 2, 384)
+    d_here, d_there = pick(d_view, x, 2), pick(d_view, 1 - x, 2)
+    d_even = jnp.stack(
+        [d_here[0], swap_seq(d_there[0], 2), swap_seq(d_here[1], 4), swap_seq(d_there[1], 6)]
+    ).reshape(4, span_rows, 2, GROUP)
+    d_even_mine = pick(d_even, core, 2)
+    d_odd = swap_seq(pick(d_even, 1 - core, 2), 1)
+    d_att = by_head(jnp.concatenate([d_even_mine, d_odd]).reshape(rows_all, GROUP)).astype(f32)
+    delta = jnp.sum(d_att * attended, axis=-1, keepdims=True) / row_sum
+    guide = (d_att / row_sum).astype(bf16)
+    d_weights = jnp.einsum("hqd,hkd->hqk", guide, values, preferred_element_type=f32)
+    d_scores = (weights * (d_weights - delta)).astype(bf16)
+    d_queries = scale * jnp.einsum("hqk,hkd->hqd", d_scores, keys, preferred_element_type=f32)
+    d_keys = scale * jnp.einsum("hqk,hqd->hkd", d_scores, queries, preferred_element_type=f32)
+    d_values = jnp.einsum("hqk,hqd->hkd", weights_low, guide, preferred_element_type=f32)
+    d_projected = jnp.concatenate(
+        [
+            turn(merged(d_queries), cosine, -sine),
+            turn(merged(d_keys), cosine, -sine),
+            merged(d_values),
+        ],
+        axis=-1,
+    ).astype(bf16)
+    d_bias_here = jnp.sum(d_projected.astype(f32), axis=0).reshape(3, 1, GROUP)
+    d_attn_bias = jnp.where(jnp.arange(4)[None, :, None] == group, d_bias_here, 0.0).reshape(-1)
+    d_weight_here = jnp.einsum("td,tf->df", rows_here, d_projected, preferred_element_type=f32)
+    d_parts = lax.all_to_all(
+        d_weight_here.astype(bf16).reshape(32, 24, 3 * GROUP), both_axes, 0, 0, tiled=True
+    )
+    d_parts = d_parts.reshape(2, 4, 4, 24, 3, GROUP).astype(f32)
+    grad_attn_weight = (
+        jnp.sum(d_parts, axis=(0, 2)).transpose(1, 2, 0, 3).reshape(24, 3 * width)
+    )
+
+    d_part = jnp.dot(d_projected, weight_here.T, preferred_element_type=f32)
+    d_part = d_part.reshape(8, span_rows, width)
+    d_blocks = d_part[:4] + swap_seq(d_part[4:].astype(bf16), 1).astype(f32)
+    d_sends = d_blocks.astype(bf16)
+    d_first = d_blocks[0] + swap_seq(d_sends[1], 2).astype(f32)
+    d_second = swap_seq(d_sends[2], 4).astype(f32) + swap_seq(d_sends[3], 6).astype(f32)
+    grad_hidden = by_sequence(d_resid_one + jnp.concatenate([d_first, d_second], axis=0), f32)
+
+    d_up_bias_all = jnp.where(
+        jnp.arange(2)[None, :, None] == core, d_up_bias.reshape(4, 1, 384), 0.0
+    ).reshape(-1)
+    d_small = jnp.concatenate(
+        [
+            d_attn_bias[: 2 * width].reshape(32, 48),
+            d_attn_bias[2 * width :].reshape(32, 24),
+            d_proj_bias.reshape(32, 24),
+            d_gain_one.reshape(32, 24),
+            d_shift_one.reshape(32, 24),
+            d_down_bias.reshape(32, 24),
+            d_gain_two.reshape(32, 24),
+            d_shift_two.reshape(32, 24),
+            d_up_bias_all.reshape(32, 96),
+        ],
+        axis=-1,
+    )
+    d_small = jnp.sum(lax.all_to_all(d_small, both_axes, 0, 0, tiled=True), axis=0)
+    d_vectors = [d_small[72 + 24 * i : 96 + 24 * i] for i in range(6)]
+    return (
+        layer_out,
+        grad_hidden,
+        grad_attn_weight,
+        d_small[:48],
+        d_small[48:72],
+        grad_proj_weight,
+        d_vectors[0],
+        d_vectors[1],
+        d_vectors[2],
+        grad_up_weight,
+        d_small[216:],
+        grad_down_weight,
+        d_vectors[3],
+        d_vectors[4],
+        d_vectors[5],
+    )
+
+
 def solution(mesh):
     in_specs = (
         P("batch", "seq", None),
@@ -355,6 +705,7 @@
         P(("seq", "batch")),
         P(("seq", "batch")),
     )
+    fits = mesh.shape["seq"] == SEQ_SIDE and mesh.shape["batch"] == BATCH_SIDE
     return jax.shard_map(
-        on_device, mesh=mesh, in_specs=in_specs, out_specs=out_specs, check_vma=False
-    )
+        split_layer if fits else on_device, mesh=mesh, in_specs=in_specs, out_specs=out_specs, check_vma=False
+    )

time: 1030 us -> 389 us (0.38)
  waiting for transfers between devices: 670 us -> 89.7 us
  starting transfers between devices: 2.76 us -> 74.5 us
  matrix products: 126 us -> 72.5 us
  blocking collectives: 83.2 us -> 44.5 us
  other arithmetic: 76.4 us -> 42.8 us
  between operations: 14.7 us -> 3.11 us
    reduce_scatter x3 -> x0, waiting for transfers between devices: 284 us -> none  [the longest x1 142 us: on_device(): lax.psum_scatter(d_down_weight, ('seq', 'batch'), scatter_dimension=0, ti...]
    all_gather x5 -> x0, waiting for transfers between devices: 190 us -> none  [the longest x1 63 us: on_device(): lax.all_gather(up_weight, ('seq', 'batch'), axis=0, tiled=True)]
    dot_general x56 -> x17, matrix products: 126 us -> 61.6 us  [the longest x1 9.93 us: split_layer(): jnp.dot(normed_low, up_here, preferred_element_type=f32) + up_bias_here]
    ppermute x16 -> x52, starting transfers between devices: 2.19 us -> 59.3 us  [the longest x40 39.8 us: swap_seq(): return lax.ppermute(value, 'seq', [(i, i ^ mask) for i in range(SEQ_SIDE)])]
    unnamed x10 -> x0, waiting for transfers between devices: 57.1 us -> none
    ppermute x16 -> x52, waiting for transfers between devices: 139 us -> 89.7 us  [the longest x40 51.2 us: swap_seq(): return lax.ppermute(value, 'seq', [(i, i ^ mask) for i in range(SEQ_SIDE)])]
    unnamed x2 -> x1, blocking collectives: 83.2 us -> 44.5 us
    convert_element_type x26 -> x16, other arithmetic: 27.2 us -> 8.61 us  [the longest x9 4.4 us: add_low(): (left.astype(jnp.float32) + right.astype(jnp.float32)).astype(jnp.bfloat16)]
  transfers between devices with their start and end apart: 25 -> 55, of which waited for: 24 -> 18; matrix products, arithmetic and copies ran while one was open for 21% -> 34% of each run, Pallas kernels for 0% -> 0%
where the time goes in v1:
time: 389 us; the launch traced here: 383 us
  waiting for transfers between devices  89.7 us (23%)
  starting transfers between devices  74.5 us (19%)
  matrix products  72.5 us (19%)
  local copies, waits for them, and re-layouts  56.1 us (14%)
  blocking collectives  44.5 us (11%)
  other arithmetic  42.8 us (11%)
    ppermute x40, waiting for transfers between devices, swap_seq(): return lax.ppermute(value, 'seq', [(i, i ^ mask) for i in range(SEQ_SIDE)])  51.2 us
    unnamed x1, blocking collectives  44.5 us
    ppermute x40, starting transfers between devices, swap_seq(): return lax.ppermute(value, 'seq', [(i, i ^ mask) for i in range(SEQ_SIDE)])  39.8 us
    ppermute x12, waiting for transfers between devices, swap_batch(): lax.ppermute(value, 'batch', [(i, i ^ mask) for i in range(BATCH_SIDE)])  38.5 us
    ppermute x12, starting transfers between devices, swap_batch(): lax.ppermute(value, 'batch', [(i, i ^ mask) for i in range(BATCH_SIDE)])  19.5 us
    unnamed x224, local copies, waits for them, and re-layouts  12 us
    sub x1, matrix products, split_layer(): weights = jnp.where(valid, jnp.exp(scores - row_max), 0.0)  10.9 us
    dot_general x1, matrix products, split_layer(): jnp.dot(normed_low, up_here, preferred_element_type=f32) + up_bias_here  9.93 us
  transfers between devices with their start and end apart: 55, of which 18 were waited for; matrix products, arithmetic and copies ran while one was open for 34% of the time, Pallas kernels for 0%

profile of v1, /device:TPU:0, one launch (start us, length us, event | category | flops | bytes accessed | tf_op | source)
XLA Modules:
  0.0 383.2 jit_solution(18105779586624901626)
XLA Ops:
  1.6 3.0 collective-permute-start.1
  6.1 3.6 collective-permute-start.20
  15.1 4.4 %all-to-all-start = ((bf16[32,24,576]{2,1,0:T(8,128)(2,1)}), bf16[32,24,576]{2,1,0:T(8,128)(2,1)}, u32[]{:S(2)}, u32[]{:S(2)}) async-start(bf16[32,24,576]{2,1,0:T(8,128)(2,1)} %bitcast.13), calls=%async_computation | async-start | bytes 1966080 | tf_op jit(solution)/shard_map/all_to_all | solution.py:460
  20.0 44.5 %all-reduce = bf16[9984]{0:T(1024)(128)(2,1)S(1)} all-reduce(bf16[9984]{0:T(1024)(128)(2,1)S(1)} %dynamic-update-slice), channel_id=2, replica_groups=mesh['seq'=8,'batch'=4] {'seq','batch'}, use_global_device_ids=true, to_apply=%add | all-reduce | flops 9984 | bytes 39936
  84.8 3.8 %collective-permute-start.23 = (bf16[2,96,768]{2,1,0:T(8,128)(2,1)S(1)}, bf16[2,96,768]{2,1,0:T(8,128)(2,1)S(1)}, u32[]{:S(2)}, u32[]{:S(2)}) collective-permute-start(bf16[2,96,768]{2,1,0:T(8,128)(2,1)S(1)} %pad_maximum_fusion.23), channel_id=1, source_target_pairs={{0,16},{4,20},{8,24},{12,28},{16,0},{20,4},{24,8},{28,12},{1,17},{... | collective-permute-start | bytes 884744 | tf_op jit(solution)/shard_map/ppermute | solution.py:331
  89.0 5.1 %collective-permute-done.10 = bf16[2,24,1920]{2,1,0:T(8,128)(2,1)S(1)} collective-permute-done((bf16[2,24,1920]{2,1,0:T(8,128)(2,1)S(1)}, bf16[2,24,1920]{2,1,0:T(8,128)(2,1)S(1)}, u32[]{:S(2)}, u32[]{:S(2)}) %collective-permute-start.10) | collective-permute-done | bytes 184352 | tf_op jit(solution)/shard_map/ppermute | solution.py:335
  99.3 6.8 %collective-permute-done.12 = bf16[96,1920]{1,0:T(8,128)(2,1)S(1)} collective-permute-done((bf16[96,1920]{1,0:T(8,128)(2,1)S(1)}, bf16[96,1920]{1,0:T(8,128)(2,1)S(1)}, u32[]{:S(2)}, u32[]{:S(2)}) %collective-permute-start.12) | collective-permute-done | bytes 368672 | tf_op jit(solution)/shard_map/ppermute | solution.py:331
  110.3 15.4 %collective-permute-done.13 = bf16[2,96,1920]{2,1,0:T(8,128)(2,1)S(1)} collective-permute-done((bf16[2,96,1920]{2,1,0:T(8,128)(2,1)S(1)}, bf16[2,96,1920]{2,1,0:T(8,128)(2,1)S(1)}, u32[]{:S(2)}, u32[]{:S(2)}) %collective-permute-start.13) | collective-permute-done | bytes 737312 | tf_op jit(solution)/shard_map/ppermute | solution.py:331
  125.9 6.2 %collective-permute-done.15 = bf16[2,96,1920]{2,1,0:T(8,128)(2,1)S(1)} collective-permute-done((bf16[2,96,1920]{2,1,0:T(8,128)(2,1)S(1)}, bf16[2,96,1920]{2,1,0:T(8,128)(2,1)S(1)}, u32[]{:S(2)}, u32[]{:S(2)}) %collective-permute-start.15) | collective-permute-done | bytes 737312 | tf_op jit(solution)/shard_map/ppermute | solution.py:331
  133.8 3.0 convolution_add_fusion.1
  139.6 10.9 %fusion.127 = (f32[3,1024]{1,0:T(4,128)S(1)}, f32[3,1024,1024]{1,2,0:T(8,128)}) fusion(pred[1024]{0:T(1024)(128)(4,1)S(1)} %fusion.86, bf16[3,1024,64]{1,2,0:T(8,128)(2,1)} %bitcast.361, bf16[3,1024,64]{1,2,0:T(8,128)(2,1)} %bitcast.363), kind=kOutput, calls=%fused_computation.352 | convolution fusion | flops 418382848 | bytes 13382656 | tf_op jit(solution)/shard_map/sub | solution.py:506
  150.4 6.9 %fusion.45 = (bf16[1024,3,64]{0,2,1:T(8,128)(2,1)S(1)}, f32[3,1024,64]{1,2,0:T(8,128)}) fusion(f32[1024,3]{0,1:T(4,128)S(1)} %bitcast.375, bf16[3,1024,64]{1,2,0:T(8,128)(2,1)S(1)} %bitcast.351, f32[3,1024,1024]{1,2,0:T(8,128)} %get-tuple-element.148), kind=kOutput, calls=%fused_computation.125 | convolution fusion | flops 406192128 | bytes 14168064 | tf_op jit(solution)/shard_map/hqk,hkd->hqd/dot_general | solution.py:510
  169.2 3.1 collective-permute-done.5
  180.6 9.9 %multiply_convert_fusion.1 = (bf16[512,1536]{1,0:T(8,128)(2,1)S(1)}, f32[512,1536]{1,0:T(8,128)}, f32[512,1536]{1,0:T(8,128)}) fusion(f32[1536]{0:T(1024)S(1)} %copy-done.85, bf16[768,1920]{1,0:T(8,128)(2,1)S(1)} %bitcast.347, bf16[256,768]{1,0:T(8,128)(2,1)S(1)} %collective-permute-done.17, bf16[256,768]{1,0:T(8,128)(2,1)S(1)} %fusion.50), kind=kOutput, calls=%fused_computation.15 | convolution fusion | flops 1261436928 | bytes 11018240 | tf_op jit(solution)/shard_map/dot_general | solution.py:541
  208.0 6.1 %convert_reduce_fusion = (f32[1536]{0:T(1024)S(1)}, bf16[512,1536]{1,0:T(8,128)(2,1)S(1)}) fusion(f32[512,1536]{1,0:T(8,128)} %get-tuple-element.37, f32[512,1536]{1,0:T(8,128)} %get-tuple-element.153, bf16[1536,768]{1,0:T(8,128)(2,1)} %bitcast.359, bf16[256,768]{1,0:T(8,128)(2,1)} %collective-permute-done.26, bf16[256,768]{1,0:T(8,128)(2,1)} %get-tuple-element.24), kind=kOutput, calls=%fused_computation.13 | convolution fusion | flops 1222113792 | bytes 11016192 | tf_op jit(solution)/shard_map/dot_general | solution.py:566
  218.1 3.0 convolution_convert_fusion
  251.4 6.7 %fusion.23 = bf16[3,1024,64]{1,2,0:T(8,128)(2,1)S(1)} fusion(f32[3,1024,1024]{1,2,0:T(8,128)} %get-tuple-element.148, f32[1024,3,64]{0,2,1:T(8,128)S(1)} %reshape.598, f32[3,1024]{1,0:T(4,128)S(1)} %get-tuple-element.147), kind=kOutput, calls=%fused_computation.63 | convolution fusion | flops 406388736 | bytes 13774848 | tf_op jit(solution)/shard_map/hqk,hqd->hkd/dot_general | solution.py:607
  258.4 6.5 %multiply_convert_fusion = bf16[3,1024,1024]{1,2,0:T(8,128)(2,1)S(1)} fusion(f32[3,1024,1024]{1,2,0:T(8,128)} %get-tuple-element.148, f32[3,1024]{1,0:T(4,128)S(1)} %div.96, bf16[3,1024,64]{1,2,0:T(8,128)(2,1)S(1)} %bitcast.352, f32[1024,3,64]{0,2,1:T(8,128)S(1)} %reshape.598, f32[3,1024]{1,0:T(4,128)S(1)} %get-tuple-element.147), kind=kOutput, calls=%fused_computation.1 | convolution fusion | flops 412483584 | bytes 20078592 | tf_op jit(solution)/shard_map/hqd,hkd->hqk/dot_general | solution.py:603
  271.0 4.4 %fusion.104 = f32[1024,768]{1,0:T(8,128)} fusion(bf16[768,576]{1,0:T(8,128)(2,1)} %bitcast.14, bf16[1024,192]{0,1:T(8,128)(2,1)S(1)} %bitcast.367, bf16[1024,192]{0,1:T(8,128)(2,1)S(1)} %get-tuple-element.104, bf16[1024,192]{0,1:T(8,128)(2,1)S(1)} %get-tuple-element.103), kind=kOutput, calls=%fused_computation.334 | convolution fusion | flops 909508608 | bytes 5210112 | tf_op jit(solution)/shard_map/dot_general | solution.py:627
  276.7 4.8 %all-to-all-start.2 = ((f32[32,1,312]{2,1,0:T(1,128)}), f32[32,1,312]{2,1,0:T(1,128)}, u32[]{:S(2)}, u32[]{:S(2)}) async-start(f32[32,1,312]{2,1,0:T(1,128)} %all_to_all.14), calls=%async_computation.2 | async-start | bytes 98304 | tf_op jit(solution)/shard_map/all_to_all | solution.py:652
  281.6 3.4 convolution_convert_fusion.3
  290.5 5.9 %all-to-all-start.1 = ((bf16[32,24,576]{2,1,0:T(8,128)(2,1)}), bf16[32,24,576]{2,1,0:T(8,128)(2,1)}, u32[]{:S(2)}, u32[]{:S(2)}) async-start(bf16[32,24,576]{2,1,0:T(8,128)(2,1)} %bitcast.105), calls=%async_computation.1 | async-start | bytes 1966080 | tf_op jit(solution)/shard_map/all_to_all | solution.py:619
  299.3 3.6 collective-permute-start.51
  310.3 10.1 %collective-permute-done.51 = bf16[96,768]{1,0:T(8,128)(2,1)S(1)} collective-permute-done((bf16[96,768]{1,0:T(8,128)(2,1)S(1)}, bf16[96,768]{1,0:T(8,128)(2,1)S(1)}, u32[]{:S(2)}, u32[]{:S(2)}) %collective-permute-start.51) | collective-permute-done | bytes 147488 | tf_op jit(solution)/shard_map/ppermute | solution.py:335
  321.9 11.8 %collective-permute-done.50 = bf16[96,768]{1,0:T(8,128)(2,1)S(1)} collective-permute-done((bf16[96,768]{1,0:T(8,128)(2,1)S(1)}, bf16[96,768]{1,0:T(8,128)(2,1)S(1)}, u32[]{:S(2)}, u32[]{:S(2)}) %collective-permute-start.50) | collective-permute-done | bytes 147488 | tf_op jit(solution)/shard_map/ppermute | solution.py:335
  337.5 4.5 %collective-permute-done.35 = bf16[128,768]{1,0:T(8,128)(2,1)S(1)} collective-permute-done((bf16[128,768]{1,0:T(8,128)(2,1)S(1)}, bf16[128,768]{1,0:T(8,128)(2,1)S(1)}, u32[]{:S(2)}, u32[]{:S(2)}) %collective-permute-start.35) | collective-permute-done | bytes 196640 | tf_op jit(solution)/shard_map/ppermute | solution.py:331
  342.0 4.1 %collective-permute-done.34 = bf16[128,768]{1,0:T(8,128)(2,1)S(1)} collective-permute-done((bf16[128,768]{1,0:T(8,128)(2,1)S(1)}, bf16[128,768]{1,0:T(8,128)(2,1)S(1)}, u32[]{:S(2)}, u32[]{:S(2)}) %collective-permute-start.34) | collective-permute-done | bytes 196640 | tf_op jit(solution)/shard_map/ppermute | solution.py:331
  349.2 7.9 %collective-permute-done.38 = bf16[96,1920]{1,0:T(8,128)(2,1)S(1)} collective-permute-done((bf16[96,1920]{1,0:T(8,128)(2,1)S(1)}, bf16[96,1920]{1,0:T(8,128)(2,1)S(1)}, u32[]{:S(2)}, u32[]{:S(2)}) %collective-permute-start.38) | collective-permute-done | bytes 368672 | tf_op jit(solution)/shard_map/ppermute | solution.py:331
  360.4 2.8 collective-permute-start.41
  363.4 4.9 %collective-permute-done.43 = bf16[2,24,1920]{2,1,0:T(8,128)(2,1)S(1)} collective-permute-done((bf16[2,24,1920]{2,1,0:T(8,128)(2,1)S(1)}, bf16[2,24,1920]{2,1,0:T(8,128)(2,1)S(1)}, u32[]{:S(2)}, u32[]{:S(2)}) %collective-permute-start.43) | collective-permute-done | bytes 184352 | tf_op jit(solution)/shard_map/ppermute | solution.py:335
  368.2 5.7 %collective-permute-done.42 = bf16[2,24,1920]{2,1,0:T(8,128)(2,1)S(1)} collective-permute-done((bf16[2,24,1920]{2,1,0:T(8,128)(2,1)S(1)}, bf16[2,24,1920]{2,1,0:T(8,128)(2,1)S(1)}, u32[]{:S(2)}, u32[]{:S(2)}) %collective-permute-start.42) | collective-permute-done | bytes 184352 | tf_op jit(solution)/shard_map/ppermute | solution.py:335
  377.7 3.2 reshape.586
  (519 shorter events, 154.1 us)
Async XLA Ops:
  1.6 83.2 %collective-permute-start.1 = (bf16[128,768]{1,0:T(8,128)(2,1)S(1)}, bf16[128,768]{1,0:T(8,128)(2,1)S(1)}, u32[]{:S(2)}, u32[]{:S(2)}) collective-permute-start(bf16[128,768]{1,0:T(8,128)(2,1)S(1)} %dynamic-slice_bitcast_fusion.12), channel_id=1, source_target_pairs={{0,16},{4,20},{8,24},{12,28},{16,0},{20,4},{24,8},{28,12},{1,17},{... | collective-permute-start | bytes 589832 | tf_op jit(solution)/shard_map/ppermute | solution.py:331
  4.6 84.0 %collective-permute-start.2 = (bf16[128,768]{1,0:T(8,128)(2,1)S(1)}, bf16[128,768]{1,0:T(8,128)(2,1)S(1)}, u32[]{:S(2)}, u32[]{:S(2)}) collective-permute-start(bf16[128,768]{1,0:T(8,128)(2,1)S(1)} %dynamic-slice_bitcast_fusion.12), channel_id=1, source_target_pairs={{0,24},{4,28},{8,16},{12,20},{16,8},{20,12},{24,0},{28,4},{1,25},{... | collective-permute-start | bytes 589832 | tf_op jit(solution)/shard_map/ppermute | solution.py:331
  6.1 68.2 %collective-permute-start.20 = (bf16[96,768]{1,0:T(8,128)(2,1)}, bf16[96,768]{1,0:T(8,128)(2,1)S(1)}, u32[]{:S(2)}, u32[]{:S(2)}) collective-permute-start(bf16[96,768]{1,0:T(8,128)(2,1)} %param.25), channel_id=1, source_target_pairs={{0,3},{1,2},{2,1},{3,0},{4,7},{5,6},{6,5},{7,4},{8,11},{9,10},{10,... | collective-permute-start | bytes 442376 | tf_op jit(solution)/shard_map/ppermute | solution.py:335
  9.7 67.0 %collective-permute-start.19 = (bf16[96,768]{1,0:T(8,128)(2,1)}, bf16[96,768]{1,0:T(8,128)(2,1)S(1)}, u32[]{:S(2)}, u32[]{:S(2)}) collective-permute-start(bf16[96,768]{1,0:T(8,128)(2,1)} %param.25), channel_id=1, source_target_pairs={{0,2},{1,3},{2,0},{3,1},{4,6},{5,7},{6,4},{7,5},{8,10},{9,11},{10,... | collective-permute-start | bytes 442376 | tf_op jit(solution)/shard_map/ppermute | solution.py:335
  12.6 61.6 %collective-permute-start.8 = (bf16[24,1920]{1,0:T(8,128)(2,1)S(1)}, bf16[24,1920]{1,0:T(8,128)(2,1)S(1)}, u32[]{:S(2)}, u32[]{:S(2)}) collective-permute-start(bf16[24,1920]{1,0:T(8,128)(2,1)S(1)} %pad_maximum_fusion.28), channel_id=1, source_target_pairs={{0,4},{4,0},{8,12},{12,8},{16,20},{20,16},{24,28},{28,24},{1,5},{5... | collective-permute-start | bytes 276488 | tf_op jit(solution)/shard_map/ppermute | solution.py:331
  15.1 118.7 %all-to-all-start = ((bf16[32,24,576]{2,1,0:T(8,128)(2,1)}), bf16[32,24,576]{2,1,0:T(8,128)(2,1)}, u32[]{:S(2)}, u32[]{:S(2)}) async-start(bf16[32,24,576]{2,1,0:T(8,128)(2,1)} %bitcast.13), calls=%async_computation | async-start | bytes 1966080 | tf_op jit(solution)/shard_map/all_to_all | solution.py:460
  76.7 12.2 %collective-permute-start.11 = (bf16[2,24,1920]{2,1,0:T(8,128)(2,1)S(1)}, bf16[2,24,1920]{2,1,0:T(8,128)(2,1)S(1)}, u32[]{:S(2)}, u32[]{:S(2)}) collective-permute-start(bf16[2,24,1920]{2,1,0:T(8,128)(2,1)S(1)} %get-tuple-element.125), channel_id=1, source_target_pairs={{0,3},{1,2},{2,1},{3,0},{4,7},{5,6},{6,5},{7,4},{8,11},{9,10},{10,... | collective-permute-start | bytes 552968 | tf_op jit(solution)/shard_map/ppermute | solution.py:335
  79.9 14.2 %collective-permute-start.10 = (bf16[2,24,1920]{2,1,0:T(8,128)(2,1)S(1)}, bf16[2,24,1920]{2,1,0:T(8,128)(2,1)S(1)}, u32[]{:S(2)}, u32[]{:S(2)}) collective-permute-start(bf16[2,24,1920]{2,1,0:T(8,128)(2,1)S(1)} %get-tuple-element.125), channel_id=1, source_target_pairs={{0,2},{1,3},{2,0},{3,1},{4,6},{5,7},{6,4},{7,5},{8,10},{9,11},{10,... | collective-permute-start | bytes 552968 | tf_op jit(solution)/shard_map/ppermute | solution.py:335
  82.1 12.0 %collective-permute-start.9 = (bf16[2,24,1920]{2,1,0:T(8,128)(2,1)S(1)}, bf16[2,24,1920]{2,1,0:T(8,128)(2,1)S(1)}, u32[]{:S(2)}, u32[]{:S(2)}) collective-permute-start(bf16[2,24,1920]{2,1,0:T(8,128)(2,1)S(1)} %get-tuple-element.125), channel_id=1, source_target_pairs={{0,1},{1,0},{2,3},{3,2},{4,5},{5,4},{6,7},{7,6},{8,9},{9,8},{10,11... | collective-permute-start | bytes 552968 | tf_op jit(solution)/shard_map/ppermute | solution.py:335
  88.9 21.4 %collective-permute-start.3 = (bf16[512,768]{1,0:T(8,128)(2,1)S(1)}, bf16[512,768]{1,0:T(8,128)(2,1)S(1)}, u32[]{:S(2)}, u32[]{:S(2)}) collective-permute-start(bf16[512,768]{1,0:T(8,128)(2,1)S(1)} %pad_maximum_fusion.4), channel_id=1, source_target_pairs={{0,4},{4,0},{8,12},{12,8},{16,20},{20,16},{24,28},{28,24},{1,5},{5... | collective-permute-start | bytes 2359304 | tf_op jit(solution)/shard_map/ppermute | solution.py:331
  95.3 12.6 %collective-permute-start.14 = (bf16[96,1920]{1,0:T(8,128)(2,1)S(1)}, bf16[96,1920]{1,0:T(8,128)(2,1)S(1)}, u32[]{:S(2)}, u32[]{:S(2)}) collective-permute-start(bf16[96,1920]{1,0:T(8,128)(2,1)S(1)} %bitcast.370), channel_id=1, source_target_pairs={{0,16},{4,20},{8,24},{12,28},{16,0},{20,4},{24,8},{28,12},{1,17},{... | collective-permute-start | bytes 1105928 | tf_op jit(solution)/shard_map/ppermute | solution.py:331
  97.7 61.6 %collective-permute-start.24 = (bf16[2,2,96,768]{3,2,1,0:T(8,128)(2,1)}, bf16[2,2,96,768]{3,2,1,0:T(8,128)(2,1)}, u32[]{:S(2)}, u32[]{:S(2)}) collective-permute-start(bf16[2,2,96,768]{3,2,1,0:T(8,128)(2,1)} %pad_maximum_fusion.13), channel_id=1, source_target_pairs={{0,8},{4,12},{8,0},{12,4},{16,24},{20,28},{24,16},{28,20},{1,9},{5... | collective-permute-start | bytes 1769480 | tf_op jit(solution)/shard_map/ppermute | solution.py:331
  106.2 19.5 %collective-permute-start.13 = (bf16[2,96,1920]{2,1,0:T(8,128)(2,1)S(1)}, bf16[2,96,1920]{2,1,0:T(8,128)(2,1)S(1)}, u32[]{:S(2)}, u32[]{:S(2)}) collective-permute-start(bf16[2,96,1920]{2,1,0:T(8,128)(2,1)S(1)} %pad_maximum_fusion.9), channel_id=1, source_target_pairs={{0,16},{4,20},{8,24},{12,28},{16,0},{20,4},{24,8},{28,12},{1,17},{... | collective-permute-start | bytes 2211848 | tf_op jit(solution)/shard_map/ppermute | solution.py:331
  108.1 24.0 %collective-permute-start.15 = (bf16[2,96,1920]{2,1,0:T(8,128)(2,1)S(1)}, bf16[2,96,1920]{2,1,0:T(8,128)(2,1)S(1)}, u32[]{:S(2)}, u32[]{:S(2)}) collective-permute-start(bf16[2,96,1920]{2,1,0:T(8,128)(2,1)S(1)} %pad_maximum_fusion.10), channel_id=1, source_target_pairs={{0,8},{4,12},{8,0},{12,4},{16,24},{20,28},{24,16},{28,20},{1,9},{5... | collective-permute-start | bytes 2211848 | tf_op jit(solution)/shard_map/ppermute | solution.py:331
  109.6 67.1 %collective-permute-start.22 = (bf16[2,2,96,768]{3,2,1,0:T(8,128)(2,1)}, bf16[2,2,96,768]{3,2,1,0:T(8,128)(2,1)}, u32[]{:S(2)}, u32[]{:S(2)}) collective-permute-start(bf16[2,2,96,768]{3,2,1,0:T(8,128)(2,1)} %pad_maximum_fusion.12), channel_id=1, source_target_pairs={{0,16},{4,20},{8,24},{12,28},{16,0},{20,4},{24,8},{28,12},{1,17},{... | collective-permute-start | bytes 1769480 | tf_op jit(solution)/shard_map/ppermute | solution.py:331
  133.8 33.4 %collective-permute-start.16 = (bf16[768,384]{1,0:T(8,128)(2,1)}, bf16[768,384]{1,0:T(8,128)(2,1)}, u32[]{:S(2)}, u32[]{:S(2)}) collective-permute-start(bf16[768,384]{1,0:T(8,128)(2,1)} %slice.346), channel_id=1, source_target_pairs={{0,4},{4,0},{8,12},{12,8},{16,20},{20,16},{24,28},{28,24},{1,5},{5... | collective-permute-start | bytes 1769480 | tf_op jit(solution)/shard_map/ppermute | solution.py:331
  222.2 23.1 %collective-permute-start.45 = (bf16[2,2,96,768]{3,2,1,0:T(8,128)(2,1)}, bf16[2,2,96,768]{3,2,1,0:T(8,128)(2,1)}, u32[]{:S(2)}, u32[]{:S(2)}) collective-permute-start(bf16[2,2,96,768]{3,2,1,0:T(8,128)(2,1)} %dynamic-slice_bitcast_fusion.3), channel_id=1, source_target_pairs={{0,16},{4,20},{8,24},{12,28},{16,0},{20,4},{24,8},{28,12},{1,17},{... | collective-permute-start | bytes 1769480 | tf_op jit(solution)/shard_map/ppermute | solution.py:331
  224.5 23.7 %collective-permute-start.47 = (bf16[2,2,96,768]{3,2,1,0:T(8,128)(2,1)}, bf16[2,2,96,768]{3,2,1,0:T(8,128)(2,1)}, u32[]{:S(2)}, u32[]{:S(2)}) collective-permute-start(bf16[2,2,96,768]{3,2,1,0:T(8,128)(2,1)} %dynamic-slice_bitcast_fusion.2), channel_id=1, source_target_pairs={{0,8},{4,12},{8,0},{12,4},{16,24},{20,28},{24,16},{28,20},{1,9},{5... | collective-permute-start | bytes 1769480 | tf_op jit(solution)/shard_map/ppermute | solution.py:331
  243.0 60.7 %collective-permute-start.36 = (bf16[768,384]{1,0:T(8,128)(2,1)}, bf16[768,384]{1,0:T(8,128)(2,1)}, u32[]{:S(2)}, u32[]{:S(2)}) collective-permute-start(bf16[768,384]{1,0:T(8,128)(2,1)} %bitcast.374), channel_id=1, source_target_pairs={{0,4},{4,0},{8,12},{12,8},{16,20},{20,16},{24,28},{28,24},{1,5},{5... | collective-permute-start | bytes 1769480 | tf_op jit(solution)/shard_map/ppermute | solution.py:331
  247.4 51.6 %collective-permute-start.46 = (bf16[2,96,768]{2,1,0:T(8,128)(2,1)}, bf16[2,96,768]{2,1,0:T(8,128)(2,1)S(1)}, u32[]{:S(2)}, u32[]{:S(2)}) collective-permute-start(bf16[2,96,768]{2,1,0:T(8,128)(2,1)} %dynamic-slice_bitcast_fusion.7), channel_id=1, source_target_pairs={{0,8},{4,12},{8,0},{12,4},{16,24},{20,28},{24,16},{28,20},{1,9},{5... | collective-permute-start | bytes 884744 | tf_op jit(solution)/shard_map/ppermute | solution.py:331
  250.2 48.8 %collective-permute-start.48 = (bf16[2,96,768]{2,1,0:T(8,128)(2,1)}, bf16[2,96,768]{2,1,0:T(8,128)(2,1)S(1)}, u32[]{:S(2)}, u32[]{:S(2)}) collective-permute-start(bf16[2,96,768]{2,1,0:T(8,128)(2,1)} %dynamic-slice_bitcast_fusion.6), channel_id=1, source_target_pairs={{0,16},{4,20},{8,24},{12,28},{16,0},{20,4},{24,8},{28,12},{1,17},{... | collective-permute-start | bytes 884744 | tf_op jit(solution)/shard_map/ppermute | solution.py:331
  276.7 13.7 %all-to-all-start.2 = ((f32[32,1,312]{2,1,0:T(1,128)}), f32[32,1,312]{2,1,0:T(1,128)}, u32[]{:S(2)}, u32[]{:S(2)}) async-start(f32[32,1,312]{2,1,0:T(1,128)} %all_to_all.14), calls=%async_computation.2 | async-start | bytes 98304 | tf_op jit(solution)/shard_map/all_to_all | solution.py:652
  287.9 19.5 %collective-permute-start.32 = (bf16[4,128,768]{2,1,0:T(8,128)(2,1)}, bf16[4,128,768]{2,1,0:T(8,128)(2,1)}, u32[]{:S(2)}, u32[]{:S(2)}) collective-permute-start(bf16[4,128,768]{2,1,0:T(8,128)(2,1)} %bitcast.99), channel_id=1, source_target_pairs={{0,4},{4,0},{8,12},{12,8},{16,20},{20,16},{24,28},{28,24},{1,5},{5... | collective-permute-start | bytes 2359304 | tf_op jit(solution)/shard_map/ppermute | solution.py:331
  290.5 87.2 %all-to-all-start.1 = ((bf16[32,24,576]{2,1,0:T(8,128)(2,1)}), bf16[32,24,576]{2,1,0:T(8,128)(2,1)}, u32[]{:S(2)}, u32[]{:S(2)}) async-start(bf16[32,24,576]{2,1,0:T(8,128)(2,1)} %bitcast.105), calls=%async_computation.1 | async-start | bytes 1966080 | tf_op jit(solution)/shard_map/all_to_all | solution.py:619
  299.3 21.1 %collective-permute-start.51 = (bf16[96,768]{1,0:T(8,128)(2,1)S(1)}, bf16[96,768]{1,0:T(8,128)(2,1)S(1)}, u32[]{:S(2)}, u32[]{:S(2)}) collective-permute-start(bf16[96,768]{1,0:T(8,128)(2,1)S(1)} %get-tuple-element.94), channel_id=1, source_target_pairs={{0,3},{1,2},{2,1},{3,0},{4,7},{5,6},{6,5},{7,4},{8,11},{9,10},{10,... | collective-permute-start | bytes 442376 | tf_op jit(solution)/shard_map/ppermute | solution.py:335
  302.9 30.8 %collective-permute-start.50 = (bf16[96,768]{1,0:T(8,128)(2,1)S(1)}, bf16[96,768]{1,0:T(8,128)(2,1)S(1)}, u32[]{:S(2)}, u32[]{:S(2)}) collective-permute-start(bf16[96,768]{1,0:T(8,128)(2,1)S(1)} %get-tuple-element.93), channel_id=1, source_target_pairs={{0,2},{1,3},{2,0},{3,1},{4,6},{5,7},{6,4},{7,5},{8,10},{9,11},{10,... | collective-permute-start | bytes 442376 | tf_op jit(solution)/shard_map/ppermute | solution.py:335
  302.9 30.8 %collective-permute-start.49 = (bf16[96,768]{1,0:T(8,128)(2,1)S(1)}, bf16[96,768]{1,0:T(8,128)(2,1)S(1)}, u32[]{:S(2)}, u32[]{:S(2)}) collective-permute-start(bf16[96,768]{1,0:T(8,128)(2,1)S(1)} %get-tuple-element.92), channel_id=1, source_target_pairs={{0,1},{1,0},{2,3},{3,2},{4,5},{5,4},{6,7},{7,6},{8,9},{9,8},{10,11... | collective-permute-start | bytes 442376 | tf_op jit(solution)/shard_map/ppermute | solution.py:335
  305.5 40.6 %collective-permute-start.37 = (bf16[2,96,1920]{2,1,0:T(8,128)(2,1)S(1)}, bf16[2,96,1920]{2,1,0:T(8,128)(2,1)S(1)}, u32[]{:S(2)}, u32[]{:S(2)}) collective-permute-start(bf16[2,96,1920]{2,1,0:T(8,128)(2,1)S(1)} %dynamic-slice_bitcast_fusion.1), channel_id=1, source_target_pairs={{0,16},{4,20},{8,24},{12,28},{16,0},{20,4},{24,8},{28,12},{1,17},{... | collective-permute-start | bytes 2211848 | tf_op jit(solution)/shard_map/ppermute | solution.py:331
  307.3 40.6 %collective-permute-start.39 = (bf16[2,96,1920]{2,1,0:T(8,128)(2,1)S(1)}, bf16[2,96,1920]{2,1,0:T(8,128)(2,1)S(1)}, u32[]{:S(2)}, u32[]{:S(2)}) collective-permute-start(bf16[2,96,1920]{2,1,0:T(8,128)(2,1)S(1)} %dynamic-slice_bitcast_fusion), channel_id=1, source_target_pairs={{0,8},{4,12},{8,0},{12,4},{16,24},{20,28},{24,16},{28,20},{1,9},{5... | collective-permute-start | bytes 2211848 | tf_op jit(solution)/shard_map/ppermute | solution.py:331
  320.4 17.1 %collective-permute-start.33 = (bf16[128,768]{1,0:T(8,128)(2,1)S(1)}, bf16[128,768]{1,0:T(8,128)(2,1)S(1)}, u32[]{:S(2)}, u32[]{:S(2)}) collective-permute-start(bf16[128,768]{1,0:T(8,128)(2,1)S(1)} %get-tuple-element.66), channel_id=1, source_target_pairs={{0,8},{4,12},{8,0},{12,4},{16,24},{20,28},{24,16},{28,20},{1,9},{5... | collective-permute-start | bytes 589832 | tf_op jit(solution)/shard_map/ppermute | solution.py:331
  360.4 13.5 %collective-permute-start.42 = (bf16[2,24,1920]{2,1,0:T(8,128)(2,1)S(1)}, bf16[2,24,1920]{2,1,0:T(8,128)(2,1)S(1)}, u32[]{:S(2)}, u32[]{:S(2)}) collective-permute-start(bf16[2,24,1920]{2,1,0:T(8,128)(2,1)S(1)} %get-tuple-element.78), channel_id=1, source_target_pairs={{0,2},{1,3},{2,0},{3,1},{4,6},{5,7},{6,4},{7,5},{8,10},{9,11},{10,... | collective-permute-start | bytes 552968 | tf_op jit(solution)/shard_map/ppermute | solution.py:335
  360.4 13.5 %collective-permute-start.41 = (bf16[2,24,1920]{2,1,0:T(8,128)(2,1)S(1)}, bf16[2,24,1920]{2,1,0:T(8,128)(2,1)S(1)}, u32[]{:S(2)}, u32[]{:S(2)}) collective-permute-start(bf16[2,24,1920]{2,1,0:T(8,128)(2,1)S(1)} %get-tuple-element.77), channel_id=1, source_target_pairs={{0,1},{1,0},{2,3},{3,2},{4,5},{5,4},{6,7},{7,6},{8,9},{9,8},{10,11... | collective-permute-start | bytes 552968 | tf_op jit(solution)/shard_map/ppermute | solution.py:335
  (129 other events, 988.0 us)

commit v2 on v0

--- a/solution.py
+++ b/solution.py
@@ -1,6 +1,10 @@
+import math
+
 import jax
 import jax.numpy as jnp
 from jax import lax
+from jax.experimental import pallas as pl
+from jax.experimental.pallas import tpu as pltpu
 from jax.sharding import PartitionSpec as P
 
 HEADS = 12
@@ -320,6 +324,862 @@
     )
 
 
+SEQ_SIDE = 8
+BATCH_SIDE = 4
+GROUP = 192
+WIDE = 256
+HERE = 3
+EVEN = (0, 2, 4, 6)
+ODD = (1, 3, 5, 7)
+CORE, X, Y, Z, PLACE, LEN_MINE, LEN_OTHER, UNIT = range(8)
+F32, BF16 = jnp.float32, jnp.bfloat16
+NN = (((1,), (0,)), ((), ()))
+NT = (((1,), (1,)), ((), ()))
+TN = (((0,), (0,)), ((), ()))
+
+
+def swap_seq(value, mask):
+    return lax.ppermute(value, "seq", [(i, i ^ mask) for i in range(SEQ_SIDE)])
+
+
+def swap_batch(value, mask):
+    return lax.ppermute(value, "batch", [(i, i ^ mask) for i in range(BATCH_SIDE)])
+
+
+def after(value, *done):
+    return lax.optimization_barrier((value,) + done)[0]
+
+
+def fence(*values):
+    return lax.optimization_barrier(values)
+
+
+def shape(dims, dtype=BF16):
+    return jax.ShapeDtypeStruct(dims, dtype)
+
+
+def call(body, outs, info, *args, scratch=(), flops=0, name=None, alone=False):
+    moved = sum(a.size * a.dtype.itemsize for a in args)
+    moved += sum(math.prod(o.shape) * o.dtype.itemsize for o in outs)
+    held = sum(math.prod(m.shape) * m.dtype.itemsize for m in scratch)
+    return pl.pallas_call(
+        body,
+        out_shape=outs,
+        in_specs=[pl.BlockSpec(memory_space=pltpu.SMEM)]
+        + [pl.BlockSpec(memory_space=pltpu.VMEM)] * len(args),
+        out_specs=[pl.BlockSpec(memory_space=pltpu.VMEM)] * len(outs),
+        scratch_shapes=[pltpu.VMEM(m.shape, m.dtype) for m in scratch],
+        compiler_params=pltpu.CompilerParams(
+            vmem_limit_bytes=60 << 20 if alone else min(56 << 20, moved + held + (16 << 20))
+        ),
+        cost_estimate=pl.CostEstimate(flops=flops, bytes_accessed=moved, transcendentals=0),
+        name=name,
+    )(info, *args)
+
+
+def dot(left, right, dims=NN):
+    return lax.dot_general(left, right, dims, preferred_element_type=F32)
+
+
+def chips(info):
+    x, y = info[X], info[Y]
+    return ((y, x), (y, 1 - x), (1 - y, x), (1 - y, 1 - x))
+
+
+def lanes(start, size):
+    return pl.ds(pl.multiple_of(start, 128), size)
+
+
+def rows(start, size, unit=16):
+    return pl.ds(pl.multiple_of(start, unit), size)
+
+
+def select_body(
+    info, hidden, up, proj, v0, v1, v2, v3, v4, v5, v6, v7, mine, other, joined, small
+):
+    y = info[Y]
+    mine[...] = hidden[y]
+    other[...] = hidden[1 - y]
+    joined[:, :3072] = up[...]
+    joined[:, 3072:] = proj[...]
+    parts = [v[...].astype(F32) for v in (v0, v1, v2, v3, v4, v5, v6, v7)]
+    row = jnp.concatenate(parts + [jnp.zeros((1, 72), F32)], axis=1)
+    small[...] = jnp.broadcast_to(row, (32, 384))
+
+
+def by_batch(info, pieces):
+    z = info[Z]
+    values = [p[...].astype(F32) for p in pieces]
+    ordered = []
+    for zz in range(4):
+        k = zz ^ z
+        low = jnp.where(k == 0, values[0], values[1])
+        high = jnp.where(k == 2, values[2], values[3])
+        ordered.append(jnp.where(k < 2, low, high))
+    return ordered
+
+
+def attn_column_body(info, p0, p1, p2, p3, out):
+    column = jnp.concatenate(by_batch(info, (p0, p1, p2, p3)), axis=0)
+    for g in range(4):
+        part = jnp.concatenate(
+            [column[:, 768 * i + GROUP * g : 768 * i + GROUP * (g + 1)] for i in range(3)], axis=1
+        ).astype(BF16)
+        out[g] = part
+        out[4 + g] = part
+
+
+def up_column_body(info, p0, p1, p2, p3, keep, sent, proj, held):
+    core = info[CORE]
+    column = jnp.concatenate(by_batch(info, (p0, p1, p2, p3)), axis=0).astype(BF16)
+    held[...] = column
+    proj[...] = column[:, 3072:]
+    for which, out in ((core, keep), (1 - core, sent)):
+        for q in range(4):
+            out[96 * (q // 2) : 96 * (q // 2 + 1), 384 * (q % 2) : 384 * (q % 2 + 1)] = held[
+                :, lanes(768 * q + 384 * which, 384)
+            ]
+
+
+def up_join_body(info, keep, came, proj, out):
+    out[0:96] = keep[:96]
+    out[96:192] = came[:96]
+    out[192:288] = keep[96:]
+    out[288:384] = came[96:]
+    out[384:480] = proj[...]
+
+
+def down_column_body(info, p0, p1, p2, p3, out):
+    z = info[Z]
+    for k, p in enumerate((p0, p1, p2, p3)):
+        out[rows((z ^ k) * 96, 96), :] = p[...]
+
+
+def attend_body(
+    info, mine, r2, r4, r6, odd, given, bias, cosine, sine, padding,
+    x_out, weight, qt_out, k_out, v_out, att_out, stats, even_low, odd_low,
+):
+    weight[:, :, GROUP:] = jnp.zeros((3, 768, WIDE - GROUP), BF16)
+    for i in range(3):
+        weight[i, :, :GROUP] = given[:, GROUP * i : GROUP * (i + 1)]
+    x_out[0:128] = mine[...]
+    x_out[128:256] = r2[...]
+    x_out[256:384] = r4[...]
+    x_out[384:512] = r6[...]
+    x_out[512:1024] = odd[...]
+    tokens = x_out[...]
+    lane = lax.broadcasted_iota(jnp.int32, (1024, WIDE), 1)
+    is_even = lane % 2 == 0
+
+    def part(i):
+        return dot(tokens, weight[i]) + bias[i : i + 1, :]
+
+    def turned(value):
+        left = pltpu.roll(value, WIDE - 1, 1)
+        right = pltpu.roll(value, 1, 1)
+        return value * cosine[...] + jnp.where(is_even, left, right) * sine[...]
+
+    query = turned(part(0)).astype(BF16).astype(F32) * (HEAD_DIM**-0.5)
+    query = jnp.where(lane == GROUP, 1.0, query).T.astype(BF16)
+    qt_out[...] = query
+    key = jnp.where(lane == GROUP, padding[...], turned(part(1))).astype(BF16)
+    k_out[...] = key
+    value = part(2).astype(BF16)
+    v_out[...] = value
+    value_t = value.astype(F32).T
+    ones = jnp.ones((16, 1024), BF16)
+    row = lax.broadcasted_iota(jnp.int32, (WIDE, WIDE), 0)
+    for h in range(HERE):
+        here = (row // HEAD_DIM == h) | (row == GROUP)
+        value_h = jnp.concatenate(
+            [value_t[HEAD_DIM * h : HEAD_DIM * (h + 1)].astype(BF16), ones], axis=0
+        )
+        for b in range(4):
+            block = qt_out[:, WIDE * b : WIDE * (b + 1)].astype(F32)
+            scores = dot(key, jnp.where(here, block, 0.0).astype(BF16))
+            top = jnp.max(scores, axis=0, keepdims=True)
+            weights = jnp.exp(scores - top).astype(BF16)
+            summed = dot(value_h, weights)
+            total = summed[HEAD_DIM : HEAD_DIM + 1]
+            att_out[HEAD_DIM * h : HEAD_DIM * (h + 1), WIDE * b : WIDE * (b + 1)] = (
+                summed[:HEAD_DIM] / total
+            )
+            stats[h : h + 1, WIDE * b : WIDE * (b + 1)] = top
+            stats[4 + h : 5 + h, WIDE * b : WIDE * (b + 1)] = total
+    low = att_out[...].T.astype(BF16)
+    for i in range(4):
+        even_low[i] = low[128 * i : 128 * (i + 1)]
+        odd_low[i] = low[512 + 128 * i : 640 + 128 * i]
+
+
+def pair_body(info, own, came, p0, p1, p2, p3):
+    for i, out in enumerate((p0, p1, p2, p3)):
+        out[...] = jnp.concatenate(
+            [own[i].astype(F32), came[i].astype(F32)], axis=1
+        ).astype(BF16)
+
+
+def proj_rows_body(info, d0, dx, dy, dd, out):
+    for i, d in enumerate((d0, dx, dy, dd)):
+        out[i] = d[384:480]
+
+
+def attn_order(info):
+    x, core = info[X], info[CORE]
+    return ((x, core), (x, 1 - core), (1 - x, core), (1 - x, 1 - core))
+
+
+def mix_body(
+    info, p0, r2, r4, r6, d0, dx, dy, dd, proj_came, mine, other, vectors,
+    normed_out, low_out, hat_out, rstd_out, rows_out, proj, held,
+):
+    core = info[CORE]
+    for j, (yy, xx) in enumerate(chips(info)):
+        held[rows((yy * 4 + xx * 2 + core) * 96, 96), :] = (d0, dx, dy, dd)[j][384:480]
+        held[rows((yy * 4 + xx * 2 + 1 - core) * 96, 96), :] = proj_came[j]
+    for i, (xx, cc) in enumerate(attn_order(info)):
+        proj[GROUP * i : GROUP * (i + 1)] = held[rows((xx * 2 + cc) * GROUP, GROUP), :]
+    rows_out[0:128, 0:384] = p0[...]
+    rows_out[0:128, 384:768] = r2[...]
+    rows_out[128:256, 0:384] = r4[...]
+    rows_out[128:256, 384:768] = r6[...]
+    tokens = jnp.concatenate([mine[...], other[...]], axis=0).astype(F32)
+    resid = tokens + dot(rows_out[...], proj[...]) + vectors[0:1, :]
+    centred = resid - jnp.mean(resid, axis=1, keepdims=True)
+    rstd = lax.rsqrt(jnp.mean(centred * centred, axis=1, keepdims=True) + EPSILON)
+    hat = centred * rstd
+    normed = hat * vectors[1:2, :] + vectors[2:3, :]
+    hat_out[...] = hat
+    rstd_out[...] = jnp.broadcast_to(rstd, (256, 128))
+    normed_out[...] = normed
+    low_out[...] = normed.astype(BF16)
+
+
+def whole_up(info, blocks, held):
+    core = info[CORE]
+    for block, (yy, xx) in zip(blocks, chips(info)):
+        for half in range(2):
+            span = slice(768 * half, 768 * (half + 1))
+            for i, cc in enumerate((core, 1 - core)):
+                held[rows((yy * 4 + xx * 2 + cc) * 96, 96), span] = block[
+                    192 * half + 96 * i : 192 * half + 96 * (i + 1)
+                ]
+
+
+def whole_down(info, blocks, held):
+    for block, (yy, xx) in zip(blocks, chips(info)):
+        held[rows((yy * 2 + xx) * 384, 384), :] = block[...]
+
+
+def gelu_parts(upward):
+    gauss = jnp.exp(-0.5 * upward * upward)
+    t = 1.0 / (1.0 + (0.3275911 * 2.0**-0.5) * jnp.abs(upward))
+    poly = t * (
+        0.127414796
+        + t * (-0.142248368 + t * (0.7107068705 + t * (-0.7265760135 + t * 0.5307027145)))
+    )
+    tail = poly * gauss
+    below = jnp.where(upward < 0, tail, 1.0 - tail)
+    return upward * below, below + upward * gauss * 0.3989422804014327
+
+
+def up_body(
+    info, low_mine, low_other, u0, ux, uy, ud, d0, dx, dy, dd, bias,
+    part_mine, part_other, active_out, slope_out, up_held, down_held,
+):
+    whole_up(info, (u0, ux, uy, ud), up_held)
+    whole_down(info, (d0, dx, dy, dd), down_held)
+    for i, low in enumerate((low_mine, low_other)):
+        upward = dot(low[...], up_held[...]) + bias[...]
+        active, slope = gelu_parts(upward)
+        active = active.astype(BF16)
+        active_out[256 * i : 256 * (i + 1)] = active
+        slope_out[256 * i : 256 * (i + 1)] = slope.astype(BF16)
+        part = dot(active, down_held[...])
+        if i == 0:
+            part_mine[...] = part
+        else:
+            part_other[...] = part.astype(BF16)
+
+
+def back_norm(d_hat, hat, rstd):
+    return rstd * (
+        d_hat
+        - jnp.mean(d_hat, axis=1, keepdims=True)
+        - hat * jnp.mean(d_hat * hat, axis=1, keepdims=True)
+    )
+
+
+def column_sum(value):
+    return jnp.sum(value, axis=0, keepdims=True)
+
+
+def norm_two_body(
+    info, part_mine, came, normed, vectors, grad, out, d_resid_out, d_low, sums,
+):
+    y = info[Y]
+    resid = normed[...] + (part_mine[...] + came[...].astype(F32) + vectors[3:4, :])
+    centred = resid - jnp.mean(resid, axis=1, keepdims=True)
+    rstd = lax.rsqrt(jnp.mean(centred * centred, axis=1, keepdims=True) + EPSILON)
+    hat = centred * rstd
+    result = (hat * vectors[4:5, :] + vectors[5:6, :]).astype(BF16)
+    out[y] = result[:128]
+    out[1 - y] = result[128:]
+    position = info[PLACE] * 128 + lax.broadcasted_iota(jnp.int32, (128, 768), 0)
+    first = jnp.where(position < info[LEN_MINE], grad[y].astype(F32), 0.0)
+    second = jnp.where(position < info[LEN_OTHER], grad[1 - y].astype(F32), 0.0)
+    cotangent = jnp.concatenate([first, second], axis=0)
+    d_resid = back_norm(cotangent * vectors[4:5, :], hat, rstd)
+    d_resid_out[...] = d_resid
+    low = d_resid.astype(BF16)
+    d_low[...] = low
+    sums[0:1] = column_sum(low.astype(F32))
+    sums[1:2] = column_sum(cotangent * hat)
+    sums[2:3] = column_sum(cotangent)
+
+
+def down_grad_body(info, active, d_mine, d_other, g0, xa, xb, ya, yb, da, db, held):
+    d_low = jnp.concatenate([d_mine[...], d_other[...]], axis=0)
+    for i in range(4):
+        held[384 * i : 384 * (i + 1)] = dot(
+            active[:, 384 * i : 384 * (i + 1)], d_low, TN
+        ).astype(BF16)
+    outs = ((g0,), (xa, xb), (ya, yb), (da, db))
+    for out, (yy, xx) in zip(outs, chips(info)):
+        base = (yy * 2 + xx) * 384
+        if len(out) == 1:
+            out[0][...] = held[rows(base, 384), :]
+        else:
+            out[0][...] = held[rows(base, 192), :]
+            out[1][...] = held[rows(base + 192, 192), :]
+
+
+def add_two_body(info, a, a_came, b, b_came, a_out, b_out):
+    a_out[...] = (a[...].astype(F32) + a_came[...].astype(F32)).astype(BF16)
+    b_out[...] = (b[...].astype(F32) + b_came[...].astype(F32)).astype(BF16)
+
+
+def add_half_body(info, x, x_came, y, y_came, x_out, y_out):
+    half = x.shape[0] // 2
+    x_out[:half] = x[:half]
+    x_out[half:] = (x[half:].astype(F32) + x_came[...].astype(F32)).astype(BF16)
+    y_out[:half] = (y[:half].astype(F32) + y_came[...].astype(F32)).astype(BF16)
+    y_out[half:] = y[half:]
+
+
+def up_grad_body(
+    info, d_mine, d_other, slope, low_mine, low_other, u0, ux, uy, ud, d0, dx, dy, dd,
+    part_mine, part_other, g0, gx, gy, gd, sums, up_held, down_held, held,
+):
+    core = info[CORE]
+    whole_up(info, (u0, ux, uy, ud), up_held)
+    whole_down(info, (d0, dx, dy, dd), down_held)
+    d_ups = []
+    total = jnp.zeros((1, 1536), F32)
+    for i, d_low in enumerate((d_mine, d_other)):
+        d_active = dot(d_low[...], down_held[...], NT)
+        d_up = (slope[256 * i : 256 * (i + 1)].astype(F32) * d_active).astype(BF16)
+        total = total + column_sum(d_up.astype(F32))
+        d_ups.append(d_up)
+        part = dot(d_up, up_held[...], NT)
+        if i == 0:
+            part_mine[...] = part
+        else:
+            part_other[...] = part.astype(BF16)
+    sums[...] = total
+    d_up = jnp.concatenate(d_ups, axis=0)
+    low = jnp.concatenate([low_mine[...], low_other[...]], axis=0)
+    held[...] = dot(low, d_up, TN).astype(BF16)
+    for out, (yy, xx) in zip((g0, gx, gy, gd), chips(info)):
+        for i, cc in enumerate((core, 1 - core)):
+            block = held[rows((yy * 4 + xx * 2 + cc) * 96, 96), :]
+            out[96 * i : 96 * (i + 1)] = block[:, :768]
+            out[192 + 96 * i : 288 + 96 * i] = block[:, 768:]
+
+
+def norm_one_body(
+    info, d_resid_two, part_mine, came, hat, rstd, vectors, rows_here, proj,
+    d_resid_out, e0, e2, e4, e6, proj_own, proj_sent, sums, held,
+):
+    core = info[CORE]
+    d_normed = d_resid_two[...] + part_mine[...] + came[...].astype(F32)
+    sums[0:1] = column_sum(d_normed * hat[...])
+    sums[1:2] = column_sum(d_normed)
+    d_resid = back_norm(d_normed * vectors[1:2, :], hat[...], rstd[:, 0:1])
+    d_resid_out[...] = d_resid
+    low = d_resid.astype(BF16)
+    sums[2:3] = column_sum(low.astype(F32))
+    d_att = dot(low, proj[...], NT).astype(BF16)
+    e0[...] = d_att[:128, :384]
+    e2[...] = d_att[:128, 384:]
+    e4[...] = d_att[128:, :384]
+    e6[...] = d_att[128:, 384:]
+    d_weight = dot(rows_here[...], low, TN).astype(BF16)
+    for i, (xx, cc) in enumerate(attn_order(info)):
+        held[rows((xx * 2 + cc) * GROUP, GROUP), :] = d_weight[GROUP * i : GROUP * (i + 1)]
+    for j, (yy, xx) in enumerate(chips(info)):
+        proj_own[j] = held[rows((yy * 4 + xx * 2 + core) * 96, 96), :]
+        proj_sent[j] = held[rows((yy * 4 + xx * 2 + 1 - core) * 96, 96), :]
+
+
+def split_core_body(info, e0, e2, e4, e6, out):
+    for i, e in enumerate((e0, e2, e4, e6)):
+        out[128 * i : 128 * (i + 1)] = e[...].astype(F32)[:, GROUP:].astype(BF16)
+
+
+def attend_back_body(
+    info, e0, e2, e4, e6, came, qt, key, value, att, stats, cosine, sine,
+    d_proj, sums, guide, weights_held, d_scores_held, dq_held, dk_held, dv_held,
+):
+    d_att = jnp.concatenate(
+        [e[...].astype(F32)[:, :GROUP] for e in (e0, e2, e4, e6)] + [came[...].astype(F32)], axis=0
+    )
+    d_att_t = d_att.T
+    product = d_att_t * att[...]
+    pieces = []
+    deltas = []
+    for h in range(HERE):
+        here = slice(HEAD_DIM * h, HEAD_DIM * (h + 1))
+        total = stats[4 + h : 5 + h, :]
+        pieces.append(d_att_t[here] / total)
+        deltas.append(column_sum(product[here]) / total)
+    pieces.append(jnp.zeros((WIDE - GROUP, 1024), F32))
+    guide[...] = jnp.concatenate(pieces, axis=0).astype(BF16)
+    key_t = key[...].astype(F32).T
+    row = lax.broadcasted_iota(jnp.int32, (WIDE, WIDE), 0)
+    dk_held[...] = jnp.zeros((1024, WIDE), F32)
+    dv_held[...] = jnp.zeros((1024, WIDE), F32)
+    dq_held[GROUP:] = jnp.zeros((WIDE - GROUP, 1024), F32)
+    wide_row = lax.broadcasted_iota(jnp.int32, (WIDE, 1024), 0)
+    for h in range(HERE):
+        mine = row // HEAD_DIM == h
+        with_pad = mine | (row == GROUP)
+        key_h = key_t[HEAD_DIM * h : HEAD_DIM * (h + 1)].astype(BF16)
+        for b in range(4):
+            span = slice(WIDE * b, WIDE * (b + 1))
+            q_block = jnp.where(with_pad, qt[:, span].astype(F32), 0.0).astype(BF16)
+            g_block = jnp.where(mine, guide[:, span].astype(F32), 0.0).astype(BF16)
+            scores = dot(key[...], q_block)
+            weights = jnp.exp(scores - stats[h : h + 1, span])
+            d_weights = dot(value[...], g_block)
+            d_scores = (weights * (d_weights - deltas[h][:, span])).astype(BF16)
+            weights_held[:, span] = weights.astype(BF16)
+            d_scores_held[:, span] = d_scores
+            dq_held[HEAD_DIM * h : HEAD_DIM * (h + 1), span] = dot(key_h, d_scores)
+        here = wide_row // HEAD_DIM == h
+        q_all = jnp.where(here, qt[...].astype(F32), 0.0).astype(BF16)
+        g_all = jnp.where(here, guide[...].astype(F32), 0.0).astype(BF16)
+        dk_held[...] += dot(d_scores_held[...], q_all, NT)
+        dv_held[...] += dot(weights_held[...], g_all, NT)
+    lane = lax.broadcasted_iota(jnp.int32, (1024, WIDE), 1)
+    is_even = lane % 2 == 0
+
+    def turned_back(value):
+        left = pltpu.roll(value, WIDE - 1, 1)
+        right = pltpu.roll(value, 1, 1)
+        return value * cosine[...] - jnp.where(is_even, left, right) * sine[...]
+
+    d_query = turned_back(dq_held[...].T * (HEAD_DIM**-0.5)).astype(BF16)
+    d_key = turned_back(dk_held[...]).astype(BF16)
+    d_value = dv_held[...].astype(BF16)
+    for i, part in enumerate((d_query, d_key, d_value)):
+        d_proj[i] = part
+        sums[i : i + 1] = column_sum(part.astype(F32))
+
+
+def attn_grad_body(info, tokens, d_proj, own, sent, held):
+    core = info[CORE]
+    parts = [dot(tokens[...], d_proj[i], TN)[:, :GROUP] for i in range(3)]
+    held[...] = jnp.concatenate(parts, axis=1).astype(BF16)
+    for j, (yy, xx) in enumerate(chips(info)):
+        own[j] = held[rows((yy * 4 + xx * 2 + core) * 96, 96), :]
+        sent[j] = held[rows((yy * 4 + xx * 2 + 1 - core) * 96, 96), :]
+
+
+def attn_pair_body(info, own, came, s0, s2, s4, s6):
+    for j, out in enumerate((s0, s2, s4, s6)):
+        out[0] = own[j]
+        out[1] = came[j]
+
+
+def attn_blocks_body(info, own, r2, r4, r6, first, s1, s2, s3, held):
+    core, x, z = info[CORE], info[X], info[Z]
+    mine = own[...].astype(F32) + r4[...].astype(F32)
+    other = r2[...].astype(F32) + r6[...].astype(F32)
+    for i, cc in enumerate((core, 1 - core)):
+        held[2 * x + cc] = mine[i]
+        held[2 * (1 - x) + cc] = other[i]
+    for k, out in enumerate((first, s1, s2, s3)):
+        here = rows((z ^ k) * 24, 24, 8)
+        blocks = [held[g, here, :] for g in range(4)]
+        for i in range(3):
+            part = jnp.concatenate([b[:, GROUP * i : GROUP * (i + 1)] for b in blocks], axis=1)
+            out[:, 768 * i : 768 * (i + 1)] = part.astype(out.dtype)
+
+
+def sum_four_body(info, first, r1, r2, r3, out):
+    out[...] = (
+        first[...] + r1[...].astype(F32) + r2[...].astype(F32) + r3[...].astype(F32)
+    )
+
+
+def hidden_grad_body(info, d_proj, weight, even_out, odd_out):
+    total = jnp.zeros((1024, 768), F32)
+    for i in range(3):
+        total = total + dot(d_proj[i], weight[i], NT)
+    even_out[...] = total[:512]
+    odd_out[...] = total[512:].astype(BF16)
+
+
+def hidden_pair_body(info, even, came, own, s2, s4, s6):
+    total = even[...] + came[...].astype(F32)
+    own[...] = total[:128]
+    s2[...] = total[128:256].astype(BF16)
+    s4[...] = total[256:384].astype(BF16)
+    s6[...] = total[384:].astype(BF16)
+
+
+def hidden_end_body(info, d_resid, own, r2, r4, r6, out):
+    y = info[Y]
+    out[y] = d_resid[:128] + own[...] + r2[...].astype(F32)
+    out[1 - y] = d_resid[128:] + r4[...].astype(F32) + r6[...].astype(F32)
+
+
+def down_blocks_body(info, own, xa, xb, ya, yb, first, s1, s2, s3, held):
+    z = info[Z]
+    held[:192] = own[:192].astype(F32) + xa[...].astype(F32) + ya[...].astype(F32)
+    held[192:] = own[192:].astype(F32) + xb[...].astype(F32) + yb[...].astype(F32)
+    first[...] = held[rows(z * 96, 96), :]
+    for k, out in ((1, s1), (2, s2), (3, s3)):
+        out[...] = held[rows((z ^ k) * 96, 96), :].astype(BF16)
+
+
+def up_blocks_body(info, own, a, b, first, s1, s2, s3, held):
+    z = info[Z]
+    held[...] = own[...].astype(F32) + a[...].astype(F32) + b[...].astype(F32)
+    for k, out in enumerate((first, s1, s2, s3)):
+        block = [held[rows(96 * i + (z ^ k) * 24, 24, 8), :] for i in range(5)]
+        out[...] = jnp.concatenate(block, axis=0).astype(out.dtype)
+
+
+def up_sum_body(info, first, r1, r2, r3, own, sent, proj_out):
+    total = first[...] + r1[...].astype(F32) + r2[...].astype(F32) + r3[...].astype(F32)
+    own[...] = jnp.concatenate([total[:24], total[48:72]], axis=1)
+    sent[...] = jnp.concatenate([total[24:48], total[72:96]], axis=1).astype(BF16)
+    proj_out[...] = total[96:]
+
+
+def up_end_body(info, own, came, up_out):
+    core = info[CORE]
+    for which, source in ((core, own), (1 - core, came)):
+        for q in range(4):
+            up_out[:, lanes(768 * q + 384 * which, 384)] = source[
+                :, 384 * q : 384 * (q + 1)
+            ].astype(F32)
+
+
+def join_body(info, g0, gx, gy, gd, p_own, p_came, o0, ox, oy, da, db):
+    proj = [(p_own[j].astype(F32) + p_came[j].astype(F32)).astype(BF16) for j in range(4)]
+    for j, (g, out) in enumerate(((g0, o0), (gx, ox), (gy, oy))):
+        out[:384] = g[...]
+        out[384:] = proj[j]
+    da[...] = gd[:240]
+    db[:144] = gd[240:]
+    db[144:] = proj[3]
+
+
+def split_layer(
+    hidden_in,
+    lengths,
+    attn_weight,
+    attn_bias,
+    proj_weight,
+    proj_bias,
+    first_gain,
+    first_shift,
+    up_weight,
+    up_bias,
+    down_weight,
+    down_bias,
+    second_gain,
+    second_shift,
+    grad_out,
+):
+    both_axes = ("seq", "batch")
+    place = lax.axis_index("seq")
+    z = lax.axis_index("batch")
+    core, x, y = place & 1, (place >> 1) & 1, place >> 2
+    group = place & 3
+    len_mine = jnp.where(y == 0, lengths[0], lengths[1])
+    len_other = jnp.where(y == 0, lengths[1], lengths[0])
+    info = jnp.stack([core, x, y, z, place, len_mine, len_other, group]).astype(jnp.int32)
+
+    attn_far = [swap_batch(attn_weight, k) for k in (1, 2, 3)]
+    small_vectors = (
+        attn_bias, proj_bias, first_gain, first_shift, down_bias, second_gain, second_shift, up_bias
+    )
+    mine, other, up_proj, small_sent = call(
+        select_body,
+        [shape((128, 768)), shape((128, 768)), shape((24, 3840)), shape((32, 384), F32)],
+        info, hidden_in, up_weight, proj_weight, *[v[None] for v in small_vectors], name="select",
+        alone=True,
+    )
+    r2, r4, r6 = swap_seq(mine, 2), swap_seq(other, 4), swap_seq(other, 6)
+    up_far = [swap_batch(up_proj, k) for k in (1, 2, 3)]
+    small_all = lax.all_to_all(small_sent[:, None], both_axes, 0, 0, tiled=True)[:, 0]
+    attn_far, r2, r4, r6, small_all, mine = fence(attn_far, r2, r4, r6, small_all, mine)
+
+    (w_sent,) = call(
+        attn_column_body, [shape((8, 96, 576))], info, attn_weight, *attn_far, name="attn_column"
+    )
+    weight_given = lax.all_to_all(w_sent, "seq", 0, 0, tiled=True).reshape(768, 576)
+    odd = swap_seq(jnp.concatenate([mine, r2, r4, r6], axis=0), 1)
+    owners = place ^ jnp.array(EVEN + ODD, jnp.int32)
+    positions = (owners[:, None] * 128 + jnp.arange(128, dtype=jnp.int32)[None, :]).reshape(-1)
+    entry = jnp.arange(WIDE)
+    frequency = 10000.0 ** (-2.0 * ((entry % HEAD_DIM) // 2).astype(F32) / HEAD_DIM)
+    angles = positions.astype(F32)[:, None] * frequency[None, :]
+    used = (entry < GROUP).astype(F32)
+    cosine = jnp.cos(angles) * used
+    sine = jnp.sin(angles) * (used * jnp.where(entry % 2 == 0, -1.0, 1.0))
+    padding = jnp.broadcast_to(
+        jnp.where(positions < len_mine, 0.0, NEG_BIG)[:, None], (1024, WIDE)
+    )
+    up_far, odd, cosine, sine, padding, small_all = fence(
+        up_far, odd, cosine, sine, padding, small_all
+    )
+
+    up_keep, up_sent, proj_column = call(
+        up_column_body, [shape((192, 768)), shape((192, 768)), shape((96, 768))],
+        info, up_proj, *up_far, scratch=[shape((96, 3840))], name="up_column",
+    )
+    (up_column,) = call(
+        up_join_body, [shape((480, 768))], info, up_keep, swap_seq(up_sent, 1), proj_column,
+        name="up_join",
+    )
+    attn_bias_all = small_all[:, :72].reshape(3, 4, GROUP)
+    bias_here = lax.dynamic_index_in_dim(attn_bias_all, group, 1, keepdims=False)
+    bias_here = jnp.pad(bias_here, ((0, 0), (0, WIDE - GROUP)))
+    vectors = small_all[:, 72:216].reshape(32, 6, 24).transpose(1, 0, 2).reshape(6, 768)
+    up_bias_all = small_all[:, 216:312].reshape(4, 2, 384)
+    up_bias_here = lax.dynamic_index_in_dim(up_bias_all, core, 1, keepdims=False).reshape(1, 1536)
+    weight_given, up_column, bias_here, vectors, up_bias_here, mine, down_weight = fence(
+        weight_given, up_column, bias_here, vectors, up_bias_here, mine, down_weight
+    )
+
+    up_x, up_y = swap_seq(up_column, 2), swap_seq(up_column, 4)
+    down_far = [swap_batch(down_weight, k) for k in (1, 2, 3)]
+    tokens_here, weight_here, query_t, key, value, attended, stats, even_low, odd_low = call(
+        attend_body,
+        [
+            shape((1024, 768)), shape((3, 768, WIDE)),
+            shape((WIDE, 1024)), shape((1024, WIDE)), shape((1024, WIDE)),
+            shape((GROUP, 1024), F32), shape((8, 1024), F32),
+            shape((4, 128, GROUP)), shape((4, 128, GROUP)),
+        ],
+        info, mine, r2, r4, r6, odd, weight_given, bias_here, cosine, sine, padding,
+        flops=8_000_000_000, name="attend", alone=True,
+    )
+    down_far, even_low, odd_low = fence(down_far, even_low, odd_low)
+
+    (down_column,) = call(
+        down_column_body, [shape((384, 768))], info, down_weight, *down_far, name="down_column"
+    )
+    p0, p1, p2, p3 = call(
+        pair_body, [shape((128, 384))] * 4, info, even_low, swap_seq(odd_low, 1), name="pair"
+    )
+    p0, p1, p2, p3, down_column, up_x, up_y = fence(p0, p1, p2, p3, down_column, up_x, up_y)
+
+    a2, a4, a6 = swap_seq(p1, 2), swap_seq(p2, 4), swap_seq(p3, 6)
+    up_da, up_db = swap_seq(up_y[:240], 2), swap_seq(up_x[240:], 4)
+    a2, a4, a6, up_da, up_db, down_column = fence(a2, a4, a6, up_da, up_db, down_column)
+
+    down_x, down_y = swap_seq(down_column, 2), swap_seq(down_column, 4)
+    up_blocks = (up_column, up_x, up_y, jnp.concatenate([up_da, up_db], axis=0))
+    (proj_rows,) = call(proj_rows_body, [shape((4, 96, 768))], info, *up_blocks, name="proj_rows")
+    proj_came = swap_seq(proj_rows, 1)
+    normed, low_mine, hat_one, rstd_one, rows_here, proj_here = call(
+        mix_body,
+        [
+            shape((256, 768), F32), shape((256, 768)), shape((256, 768), F32),
+            shape((256, 128), F32), shape((256, 768)), shape((768, 768)),
+        ],
+        info, p0, a2, a4, a6, *up_blocks, proj_came, mine, other, vectors,
+        scratch=[shape((768, 768))], flops=300_000_000, name="mix",
+    )
+    low_other = swap_seq(low_mine, 1)
+    down_x, down_y, low_other = fence(down_x, down_y, low_other)
+    down_da, down_db = swap_seq(down_y[:192], 2), swap_seq(down_x[192:], 4)
+    down_blocks = (down_column, down_x, down_y, jnp.concatenate([down_da, down_db], axis=0))
+
+    part_mine, part_other, active, slope = call(
+        up_body,
+        [shape((256, 768), F32), shape((256, 768)), shape((512, 1536)), shape((512, 1536))],
+        info, low_mine, low_other, *up_blocks, *down_blocks, up_bias_here,
+        scratch=[shape((768, 1536)), shape((1536, 768))], flops=2_400_000_000, name="up",
+    )
+    layer_out, d_resid_two, d_low, sums_two = call(
+        norm_two_body,
+        [shape((2, 128, 768)), shape((256, 768), F32), shape((256, 768)), shape((8, 768), F32)],
+        info, part_mine, swap_seq(part_other, 1), normed, vectors, grad_out, name="norm_two",
+    )
+    d_came = swap_seq(d_low, 1)
+    g_down, gxa, gxb, gya, gyb, gda, gdb = call(
+        down_grad_body, [shape((384, 768))] + [shape((192, 768))] * 6, info, active, d_low, d_came,
+        scratch=[shape((1536, 768))], flops=1_200_000_000, name="down_grad",
+    )
+    gxa, gxb, gya, gyb, gda, gdb, d_low, d_came = fence(gxa, gxb, gya, gyb, gda, gdb, d_low, d_came)
+
+    gda, gdb = swap_seq(gda, 2), swap_seq(gdb, 4)
+    part_mine, part_other, g0, gx, gy, gd, up_sums = call(
+        up_grad_body,
+        [shape((256, 768), F32), shape((256, 768))] + [shape((384, 768))] * 4
+        + [shape((1, 1536), F32)],
+        info, d_low, d_came, slope, low_mine, low_other, *up_blocks, *down_blocks,
+        scratch=[shape((768, 1536)), shape((1536, 768)), shape((768, 1536))],
+        flops=3_600_000_000, name="up_grad",
+    )
+    gda, gdb, part_mine, part_other, gxa, gyb = fence(gda, gdb, part_mine, part_other, gxa, gyb)
+    gxa, gyb = swap_seq(gxa, 2), swap_seq(gyb, 4)
+    d_resid_one, e0, e2, e4, e6, proj_own, proj_sent, sums_one = call(
+        norm_one_body,
+        [shape((256, 768), F32)] + [shape((128, 384))] * 4 + [shape((4, 96, 768))] * 2
+        + [shape((8, 768), F32)],
+        info, d_resid_two, part_mine, swap_seq(part_other, 1), hat_one, rstd_one, vectors,
+        rows_here, proj_here,
+        scratch=[shape((768, 768))], flops=600_000_000, name="norm_one",
+    )
+    gxa, gyb, e0, e2, e4, e6, proj_sent = fence(gxa, gyb, e0, e2, e4, e6, proj_sent)
+
+    e2, e4, e6 = swap_seq(e2, 2), swap_seq(e4, 4), swap_seq(e6, 6)
+    proj_came = swap_seq(proj_sent, 1)
+    gxb, gya = call(
+        add_two_body, [shape((192, 768))] * 2, info, gxb, gdb, gya, gda, name="down_add"
+    )
+    j0, jx, jy, jda, jdb = call(
+        join_body, [shape((480, 768))] * 3 + [shape((240, 768))] * 2,
+        info, g0, gx, gy, gd, proj_own, proj_came, name="join",
+    )
+    (split,) = call(split_core_body, [shape((512, GROUP))], info, e0, e2, e4, e6, name="split")
+    e_came = swap_seq(split, 1)
+    e2, e4, e6, e_came, gxb, gya, jda, jdb = fence(e2, e4, e6, e_came, gxb, gya, jda, jdb)
+
+    jda, jdb = swap_seq(jda, 2), swap_seq(jdb, 4)
+    gxb, gya = swap_seq(gxb, 2), swap_seq(gya, 4)
+    d_proj, sums_attn = call(
+        attend_back_body,
+        [shape((3, 1024, WIDE)), shape((8, WIDE), F32)],
+        info, e0, e2, e4, e6, e_came, query_t, key, value, attended, stats, cosine, sine,
+        scratch=[
+            shape((WIDE, 1024)), shape((1024, 1024)), shape((1024, 1024)),
+            shape((WIDE, 1024), F32), shape((1024, WIDE), F32), shape((1024, WIDE), F32),
+        ],
+        flops=8_000_000_000, name="attend_back",
+    )
+    wg_own, wg_sent = call(
+        attn_grad_body, [shape((4, 96, 576))] * 2, info, tokens_here, d_proj,
+        scratch=[shape((768, 576))], flops=1_200_000_000, name="attn_grad",
+    )
+    even, odd_sent = call(
+        hidden_grad_body, [shape((512, 768), F32), shape((512, 768))], info, d_proj, weight_here,
+        flops=1_200_000_000, name="hidden_grad",
+    )
+    jda, jdb, gxb, gya, wg_sent, odd_sent = fence(jda, jdb, gxb, gya, wg_sent, odd_sent)
+
+    wg_came, odd_came = swap_seq(wg_sent, 1), swap_seq(odd_sent, 1)
+    jx, jy = call(add_half_body, [shape((480, 768))] * 2, info, jx, jdb, jy, jda, name="up_add")
+    first, b1, b2, b3 = call(
+        down_blocks_body, [shape((96, 768), F32)] + [shape((96, 768))] * 3,
+        info, g_down, gxa, gxb, gya, gyb, scratch=[shape((384, 768), F32)], name="down_blocks",
+    )
+    wg_came, odd_came, jx, jy, b1, b2, b3 = fence(wg_came, odd_came, jx, jy, b1, b2, b3)
+
+    jx, jy = swap_seq(jx, 2), swap_seq(jy, 4)
+    b1, b2, b3 = [swap_batch(b, k) for k, b in ((1, b1), (2, b2), (3, b3))]
+    h0, h2, h4, h6 = call(
+        attn_pair_body, [shape((2, 96, 576))] * 4, info, wg_own, wg_came, name="attn_pair",
+    )
+    own, s2, s4, s6 = call(
+        hidden_pair_body, [shape((128, 768), F32)] + [shape((128, 768))] * 3,
+        info, even, odd_came, name="hidden_pair",
+    )
+    is_group = (jnp.arange(4) == group)[None, :, None]
+    d_attn_bias = jnp.where(is_group, sums_attn[:3, None, :GROUP], 0.0).reshape(-1)
+    is_core = (jnp.arange(2) == core)[None, :, None]
+    d_up_bias = jnp.where(is_core, up_sums.reshape(4, 1, 384), 0.0).reshape(32, 96)
+    d_six = jnp.stack(
+        [sums_one[2], sums_one[0], sums_one[1], sums_two[0], sums_two[1], sums_two[2]]
+    )
+    d_small = jnp.concatenate(
+        [
+            d_attn_bias[:1536].reshape(32, 48),
+            d_attn_bias[1536:].reshape(32, 24),
+            d_six.reshape(6, 32, 24).transpose(1, 0, 2).reshape(32, 144),
+            d_up_bias,
+        ],
+        axis=-1,
+    )
+    d_small = lax.all_to_all(d_small[:, None], both_axes, 0, 0, tiled=True)
+    jx, jy, h2, h4, h6, s2, s4, s6, b1, b2, b3, d_small = fence(
+        jx, jy, h2, h4, h6, s2, s4, s6, b1, b2, b3, d_small
+    )
+
+    up_first, c1, c2, c3 = call(
+        up_blocks_body, [shape((120, 768), F32)] + [shape((120, 768))] * 3,
+        info, j0, jx, jy, scratch=[shape((480, 768), F32)], name="up_blocks",
+    )
+    c1, c2, c3 = [swap_batch(c, k) for k, c in ((1, c1), (2, c2), (3, c3))]
+    h2, h4, h6 = swap_seq(h2, 2), swap_seq(h4, 4), swap_seq(h6, 6)
+    h2, h4, h6, c1, s2, s4, s6 = fence(h2, h4, h6, c1, s2, s4, s6)
+
+    s2, s4 = swap_seq(s2, 2), swap_seq(s4, 4)
+    attn_first, *attn_sends = call(
+        attn_blocks_body, [shape((24, 2304), F32)] + [shape((24, 2304))] * 3,
+        info, h0, h2, h4, h6, scratch=[shape((4, 96, 576), F32)], name="attn_blocks",
+    )
+    c2, c3, s2, s4, s6, attn_sends = fence(c2, c3, s2, s4, s6, attn_sends)
+
+    attn_came = [swap_batch(part, k) for k, part in zip((1, 2, 3), attn_sends)]
+    s6 = swap_seq(s6, 6)
+    up_own, up_sent, grad_proj_weight = call(
+        up_sum_body, [shape((24, 1536), F32), shape((24, 1536)), shape((24, 768), F32)],
+        info, up_first, c1, c2, c3, name="up_sum",
+    )
+    (grad_up_weight,) = call(
+        up_end_body, [shape((24, 3072), F32)], info, up_own, swap_seq(up_sent, 1), name="up_end"
+    )
+    (grad_down_weight,) = call(
+        sum_four_body, [shape((96, 768), F32)], info, first, b1, b2, b3, name="down_end"
+    )
+    (grad_attn_weight,) = call(
+        sum_four_body, [shape((24, 2304), F32)], info, attn_first, *attn_came, name="attn_end"
+    )
+    (grad_hidden,) = call(
+        hidden_end_body, [shape((2, 128, 768), F32)], info, d_resid_one, own, s2, s4, s6,
+        name="hidden_end",
+    )
+
+    d_small = jnp.sum(d_small[:, 0], axis=0)
+    d_vectors = [d_small[72 + 24 * i : 96 + 24 * i] for i in range(6)]
+    return (
+        layer_out,
+        grad_hidden,
+        grad_attn_weight,
+        d_small[:48],
+        d_small[48:72],
+        grad_proj_weight,
+        d_vectors[0],
+        d_vectors[1],
+        d_vectors[2],
+        grad_up_weight,
+        d_small[216:],
+        grad_down_weight,
+        d_vectors[3],
+        d_vectors[4],
+        d_vectors[5],
+    )
+
+
 def solution(mesh):
     in_specs = (
         P("batch", "seq", None),
@@ -355,6 +1215,7 @@
         P(("seq", "batch")),
         P(("seq", "batch")),
     )
+    fits = mesh.shape["seq"] == SEQ_SIDE and mesh.shape["batch"] == BATCH_SIDE
     return jax.shard_map(
-        on_device, mesh=mesh, in_specs=in_specs, out_specs=out_specs, check_vma=False
-    )
+        split_layer if fits else on_device, mesh=mesh, in_specs=in_specs, out_specs=out_specs, check_vma=False
+    )

time: 1030 us -> 281 us (0.27)
  waiting for transfers between devices: 670 us -> 78.5 us
  matrix products: 126 us -> 0 us
  blocking collectives: 83.2 us -> 0 us
  starting transfers between devices: 2.76 us -> 85.9 us
  Pallas kernels: 0 us -> 74.6 us
  other arithmetic: 76.4 us -> 9.41 us
  local copies, waits for them, and re-layouts: 51.9 us -> 25.3 us
  between operations: 14.7 us -> 4.3 us
    reduce_scatter x3 -> x0, waiting for transfers between devices: 284 us -> none  [the longest x1 142 us: on_device(): lax.psum_scatter(d_down_weight, ('seq', 'batch'), scatter_dimension=0, ti...]
    all_gather x5 -> x0, waiting for transfers between devices: 190 us -> none  [the longest x1 63 us: on_device(): lax.all_gather(up_weight, ('seq', 'batch'), axis=0, tiled=True)]
    dot_general x56 -> x0, matrix products: 126 us -> none  [the longest x8 22.1 us: back_step(): jnp.einsum('shqk,skhd->sqhd', d_scores, keys_part, preferred_element_type...]
    unnamed x2 -> x0, blocking collectives: 83.2 us -> none
    pallas_call x0 -> x31, Pallas kernels: none -> 74.6 us  [call(): pl.pallas_call(body, out_shape=outs, in_specs=[pl.BlockSpec(memory_space=...]
    ppermute x16 -> x64, starting transfers between devices: 2.19 us -> 76.5 us  [the longest x46 38.6 us: swap_seq(): return lax.ppermute(value, 'seq', [(i, i ^ mask) for i in range(SEQ_SIDE)])]
    ppermute x16 -> x64, waiting for transfers between devices: 139 us -> 66.6 us  [the longest x46 47.8 us: swap_seq(): return lax.ppermute(value, 'seq', [(i, i ^ mask) for i in range(SEQ_SIDE)])]
    unnamed x10 -> x0, waiting for transfers between devices: 57.1 us -> none
  transfers between devices with their start and end apart: 25 -> 67, of which waited for: 24 -> 23; matrix products, arithmetic and copies ran while one was open for 21% -> 7% of each run, Pallas kernels for 0% -> 22%
where the time goes in v2:
time: 281 us; the launch traced here: 278 us
  starting transfers between devices  85.9 us (31%)
  waiting for transfers between devices  78.5 us (28%)
  Pallas kernels  74.6 us (27%)
  local copies, waits for them, and re-layouts  25.3 us (9%)
  other arithmetic  9.41 us (3%)
  between operations  4.3 us (2%)
    pallas_call x31, Pallas kernels, call(): pl.pallas_call(body, out_shape=outs, in_specs=[pl.BlockSpec(memory_space=...  74.6 us
    ppermute x46, waiting for transfers between devices, swap_seq(): return lax.ppermute(value, 'seq', [(i, i ^ mask) for i in range(SEQ_SIDE)])  47.8 us
    ppermute x46, starting transfers between devices, swap_seq(): return lax.ppermute(value, 'seq', [(i, i ^ mask) for i in range(SEQ_SIDE)])  38.6 us
    ppermute x18, starting transfers between devices, swap_batch(): lax.ppermute(value, 'batch', [(i, i ^ mask) for i in range(BATCH_SIDE)])  37.8 us
    ppermute x18, waiting for transfers between devices, swap_batch(): lax.ppermute(value, 'batch', [(i, i ^ mask) for i in range(BATCH_SIDE)])  18.8 us
    unnamed x107, local copies, waits for them, and re-layouts  14.4 us
    all_to_all x1, waiting for transfers between devices, split_layer(): d_small = lax.all_to_all(d_small[:, None], both_axes, 0, 0, tiled=True)  6.13 us
    mul x2, other arithmetic, split_layer(): sine = jnp.sin(angles) * (used * jnp.where(entry % 2 == 0, -1.0, 1.0))  5.79 us
  transfers between devices with their start and end apart: 67, of which 23 were waited for; matrix products, arithmetic and copies ran while one was open for 7% of the time, Pallas kernels for 22%

profile of v2, /device:TPU:0, one launch (start us, length us, event | category | flops | bytes accessed | tf_op | source)
XLA Modules:
  0.0 278.0 jit_solution(15973001463320672592)
XLA Ops:
  0.7 4.1 %collective-permute-start.1 = (bf16[24,2304]{1,0:T(8,128)(2,1)}, bf16[24,2304]{1,0:T(8,128)(2,1)S(1)}, u32[]{:S(2)}, u32[]{:S(2)}) collective-permute-start(bf16[24,2304]{1,0:T(8,128)(2,1)} %p0.1), channel_id=1, source_target_pairs={{0,2},{1,3},{2,0},{3,1},{4,6},{5,7},{6,4},{7,5},{8,10},{9,11},{10,... | collective-permute-start | bytes 331784 | tf_op jit(solution)/shard_map/ppermute | solution.py:346
  12.9 2.4 collective-permute-start.5
  17.3 2.6 all-to-all-start
  22.2 3.5 %collective-permute-start.2 = (bf16[24,2304]{1,0:T(8,128)(2,1)}, bf16[24,2304]{1,0:T(8,128)(2,1)S(1)}, u32[]{:S(2)}, u32[]{:S(2)}) collective-permute-start(bf16[24,2304]{1,0:T(8,128)(2,1)} %p0.1), channel_id=1, source_target_pairs={{0,3},{1,2},{2,1},{3,0},{4,7},{5,6},{6,5},{7,4},{8,11},{9,10},{10,... | collective-permute-start | bytes 331784 | tf_op jit(solution)/shard_map/ppermute | solution.py:346
  29.2 9.2 %collective-permute-start.7 = (bf16[24,3840]{1,0:T(8,128)(2,1)}, bf16[24,3840]{1,0:T(8,128)(2,1)S(1)}, u32[]{:S(2)}, u32[]{:S(2)}) collective-permute-start(bf16[24,3840]{1,0:T(8,128)(2,1)} %get-tuple-element.228.p0), channel_id=1, source_target_pairs={{0,2},{1,3},{2,0},{3,1},{4,6},{5,7},{6,4},{7,5},{8,10},{9,11},{10,... | collective-permute-start | bytes 552968 | tf_op jit(solution)/shard_map/ppermute | solution.py:346
  41.5 3.6 %all-to-all-start.1 = ((bf16[8,96,576]{2,1,0:T(8,128)(2,1)}), bf16[8,96,576]{2,1,0:T(8,128)(2,1)S(1)}, u32[]{:S(2)}, u32[]{:S(2)}) async-start(bf16[8,96,576]{2,1,0:T(8,128)(2,1)} %attn_column.1), calls=%async_computation.1 | async-start | bytes 1966080 | tf_op jit(solution)/shard_map/all_to_all | solution.py:935
  45.1 5.8 %fusion.1 = (f32[1024,256]{1,0:T(8,128)}, f32[1024,256]{1,0:T(8,128)}) fusion(f32[256]{0:T(256)S(1)} %get-tuple-element.440, f32[256]{0:T(256)S(1)} %get-tuple-element.441, f32[1024]{0:T(1024)S(1)} %convert_bitcast_fusion, f32[256]{0:T(256)S(1)} %fusion.4), kind=kLoop, calls=%fused_computation.3 | loop fusion | flops 786432 | bytes 2104320 | tf_op jit(solution)/shard_map/mul | solution.py:944
  55.5 4.2 %all-to-all-done.1 = bf16[8,96,576]{2,1,0:T(8,128)(2,1)S(1)} async-done(((bf16[8,96,576]{2,1,0:T(8,128)(2,1)}), bf16[8,96,576]{2,1,0:T(8,128)(2,1)S(1)}, u32[]{:S(2)}, u32[]{:S(2)}) %all-to-all-start.1) | async-done | bytes 884768 | tf_op jit(solution)/shard_map/all_to_all | solution.py:935
  65.2 13.8 %attend.1 = (bf16[1024,768]{1,0:T(8,128)(2,1)}, bf16[3,768,256]{2,1,0:T(8,128)(2,1)}, bf16[256,1024]{1,0:T(8,128)(2,1)}, bf16[1024,256]{1,0:T(8,128)(2,1)}, bf16...) custom-call(s32[8]{0:T(128)} %stack.39.info, ...), custom_call_target="tpu_custom_call" | custom-call | flops 8000000000 | bytes 11144192 | tf_op jit(solution)/shard_map/attend/pallas_call | solution.py:365
  86.8 2.3 collective-permute-start.19
  89.1 8.5 %collective-permute-done.17.r2 = bf16[128,384]{1,0:T(8,128)(2,1)S(1)} collective-permute-done((bf16[128,384]{1,0:T(8,128)(2,1)S(1)}, bf16[128,384]{1,0:T(8,128)(2,1)S(1)}, u32[]{:S(2)}, u32[]{:S(2)}) %collective-permute-start.17) | collective-permute-done | bytes 98336 | tf_op jit(solution)/shard_map/ppermute | solution.py:342
  104.0 11.3 %collective-permute-done.24.dy = bf16[384,768]{1,0:T(8,128)(2,1)S(1)} collective-permute-done((bf16[384,768]{1,0:T(8,128)(2,1)S(1)}, bf16[384,768]{1,0:T(8,128)(2,1)S(1)}, u32[]{:S(2)}, u32[]{:S(2)}) %collective-permute-start.24) | collective-permute-done | bytes 589856 | tf_op jit(solution)/shard_map/ppermute | solution.py:342
  118.6 6.1 %collective-permute-done.26 = bf16[192,768]{1,0:T(8,128)(2,1)S(1)} collective-permute-done((bf16[192,768]{1,0:T(8,128)(2,1)S(1)}, bf16[192,768]{1,0:T(8,128)(2,1)S(1)}, u32[]{:S(2)}, u32[]{:S(2)}) %collective-permute-start.26) | collective-permute-done | bytes 294944 | tf_op jit(solution)/shard_map/ppermute | solution.py:342
  126.1 5.3 %up.3 = (f32[256,768]{1,0:T(8,128)S(1)}, bf16[256,768]{1,0:T(8,128)(2,1)S(1)}, bf16[512,1536]{1,0:T(8,128)(2,1)S(1)}, bf16[512,1536]{1,0:T(8,128)(2,1)S(1)}) custom-call(s32[8]{0:T(128)S(1)} %copy-done.17, bf16[256,768]{1,0:T(8,128)(2,1)S(1)} %get-tuple-element.274.low_mine, bf16[256,768]{1,0:T(8,128)(2,1)S(1)} %collective-permute-done.25.low_other, ...), custom_call_target="tpu_custom_call" | custom-call | flops 2400000000 | bytes 10426368 | tf_op jit(solution)/shard_map/up/pallas_call | solution.py:365
  140.9 4.9 %up_grad.1 = (f32[256,768]{1,0:T(8,128)S(1)}, bf16[256,768]{1,0:T(8,128)(2,1)S(1)}, bf16[384,768]{1,0:T(8,128)(2,1)S(1)}, bf16[384,768]{1,0:T(8,128)(2,1)S(1)}, ...) custom-call(s32[8]{0:T(128)S(1)} %copy-done.17, ...), custom_call_target="tpu_custom_call" | custom-call | flops 3600000000 | bytes 11999232 | tf_op jit(solution)/shard_map/up_grad/pallas_call | solution.py:365
  145.9 3.0 %collective-permute-done.30.b_came = bf16[192,768]{1,0:T(8,128)(2,1)S(1)} collective-permute-done((bf16[192,768]{1,0:T(8,128)(2,1)S(1)}, bf16[192,768]{1,0:T(8,128)(2,1)S(1)}, u32[]{:S(2)}, u32[]{:S(2)}) %collective-permute-start.30) | collective-permute-done | bytes 294944 | tf_op jit(solution)/shard_map/ppermute | solution.py:342
  151.2 2.3 norm_one.1
  153.5 4.9 %collective-permute-done.33.xa = bf16[192,768]{1,0:T(8,128)(2,1)S(1)} collective-permute-done((bf16[192,768]{1,0:T(8,128)(2,1)S(1)}, bf16[192,768]{1,0:T(8,128)(2,1)S(1)}, u32[]{:S(2)}, u32[]{:S(2)}) %collective-permute-start.33) | collective-permute-done | bytes 294944 | tf_op jit(solution)/shard_map/ppermute | solution.py:342
  160.9 2.3 collective-permute-start.37
  176.5 9.7 %attend_back.1 = (bf16[3,1024,256]{2,1,0:T(8,128)(2,1)S(1)}, f32[8,256]{1,0:T(8,128)S(1)}) custom-call(s32[8]{0:T(128)S(1)} %copy-done.17, bf16[128,384]{1,0:T(8,128)(2,1)S(1)} %get-tuple-element.316.e0, bf16[128,384]{1,0:T(8,128)(2,1)S(1)} %collective-permute-done.35.e2, bf16[128,384]{1,0:T(8,128)(2,1)S(1)} %collective-permute-done.36.e4, ...), custom_call_target="tpu_custom_call" | custom-call | flops 8000000000 | bytes 6660096 | tf_op jit(solution)/shard_map/attend_back/pallas_call | solution.py:365
  186.2 2.9 %attn_grad.1 = (bf16[4,96,576]{2,1,0:T(8,128)(2,1)S(1)}, bf16[4,96,576]{2,1,0:T(8,128)(2,1)}) custom-call(s32[8]{0:T(128)S(1)} %copy-done.17, bf16[1024,768]{1,0:T(8,128)(2,1)S(1)} %copy-done.39, bf16[3,1024,256]{2,1,0:T(8,128)(2,1)S(1)} %get-tuple-element.343.d_proj), custom_call_target="tpu_custom_call" | custom-call | flops 1200000000 | bytes 4030464 | tf_op jit(solution)/shard_map/attn_grad/pallas_call | solution.py:365
  189.1 3.0 %hidden_grad.1 = (f32[512,768]{1,0:T(8,128)S(1)}, bf16[512,768]{1,0:T(8,128)(2,1)}) custom-call(s32[8]{0:T(128)S(1)} %copy-done.17, bf16[3,1024,256]{2,1,0:T(8,128)(2,1)S(1)} %get-tuple-element.343.d_proj, bf16[3,768,256]{2,1,0:T(8,128)(2,1)S(1)} %copy-done.40), custom_call_target="tpu_custom_call" | custom-call | flops 1200000000 | bytes 5111808 | tf_op jit(solution)/shard_map/hidden_grad/pallas_call | solution.py:365
  209.8 2.4 collective-permute-start.50
  213.0 3.3 %all-to-all-start.2 = ((f32[32,1,312]{2,1,0:T(1,128)}), f32[32,1,312]{2,1,0:T(1,128)}, u32[]{:S(2)}, u32[]{:S(2)}) async-start(f32[32,1,312]{2,1,0:T(1,128)} %broadcast_in_dim.124), calls=%async_computation.2 | async-start | bytes 98304 | tf_op jit(solution)/shard_map/all_to_all | solution.py:1122
  220.1 6.1 %all-to-all-done.2 = f32[32,1,312]{2,1,0:T(1,128)} async-done(((f32[32,1,312]{2,1,0:T(1,128)}), f32[32,1,312]{2,1,0:T(1,128)}, u32[]{:S(2)}, u32[]{:S(2)}) %all-to-all-start.2) | async-done | bytes 39968 | tf_op jit(solution)/shard_map/all_to_all | solution.py:1122
  230.9 2.7 up_blocks.1
  234.2 5.2 %collective-permute-done.56.r1 = bf16[120,768]{1,0:T(8,128)(2,1)S(1)} collective-permute-done((bf16[120,768]{1,0:T(8,128)(2,1)S(1)}, bf16[120,768]{1,0:T(8,128)(2,1)S(1)}, u32[]{:S(2)}, u32[]{:S(2)}) %collective-permute-start.56) | collective-permute-done | bytes 184352 | tf_op jit(solution)/shard_map/ppermute | solution.py:346
  243.0 2.3 collective-permute-start.52
  247.1 9.3 %collective-permute-done.51.r2 = bf16[120,768]{1,0:T(8,128)(2,1)} collective-permute-done((bf16[120,768]{1,0:T(8,128)(2,1)}, bf16[120,768]{1,0:T(8,128)(2,1)}, u32[]{:S(2)}, u32[]{:S(2)}) %collective-permute-start.51) | collective-permute-done | bytes 184352 | tf_op jit(solution)/shard_map/ppermute | solution.py:346
  259.0 4.4 %collective-permute-start.60 = (bf16[24,2304]{1,0:T(8,128)(2,1)S(1)}, bf16[24,2304]{1,0:T(8,128)(2,1)S(1)}, u32[]{:S(2)}, u32[]{:S(2)}) collective-permute-start(bf16[24,2304]{1,0:T(8,128)(2,1)S(1)} %get-tuple-element.414), channel_id=1, source_target_pairs={{0,1},{1,0},{2,3},{3,2},{4,5},{5,4},{6,7},{7,6},{8,9},{9,8},{10,11... | collective-permute-start | bytes 331784 | tf_op jit(solution)/shard_map/ppermute | solution.py:346
  263.5 2.4 collective-permute-start.62
  271.9 3.1 %collective-permute-done.61.r2 = bf16[24,2304]{1,0:T(8,128)(2,1)S(1)} collective-permute-done((bf16[24,2304]{1,0:T(8,128)(2,1)S(1)}, bf16[24,2304]{1,0:T(8,128)(2,1)S(1)}, u32[]{:S(2)}, u32[]{:S(2)}) %collective-permute-start.61) | collective-permute-done | bytes 110624 | tf_op jit(solution)/shard_map/ppermute | solution.py:346
  (295 shorter events, 116.7 us)
Async XLA Ops:
  0.7 21.6 %collective-permute-start.1 = (bf16[24,2304]{1,0:T(8,128)(2,1)}, bf16[24,2304]{1,0:T(8,128)(2,1)S(1)}, u32[]{:S(2)}, u32[]{:S(2)}) collective-permute-start(bf16[24,2304]{1,0:T(8,128)(2,1)} %p0.1), channel_id=1, source_target_pairs={{0,2},{1,3},{2,0},{3,1},{4,6},{5,7},{6,4},{7,5},{8,10},{9,11},{10,... | collective-permute-start | bytes 331784 | tf_op jit(solution)/shard_map/ppermute | solution.py:346
  4.8 22.6 %collective-permute-start = (bf16[24,2304]{1,0:T(8,128)(2,1)}, bf16[24,2304]{1,0:T(8,128)(2,1)S(1)}, u32[]{:S(2)}, u32[]{:S(2)}) collective-permute-start(bf16[24,2304]{1,0:T(8,128)(2,1)} %p0.1), channel_id=1, source_target_pairs={{0,1},{1,0},{2,3},{3,2},{4,5},{5,4},{6,7},{7,6},{8,9},{9,8},{10,11... | collective-permute-start | bytes 331784 | tf_op jit(solution)/shard_map/ppermute | solution.py:346
  12.9 25.5 %collective-permute-start.5 = (bf16[128,768]{1,0:T(8,128)(2,1)}, bf16[128,768]{1,0:T(8,128)(2,1)S(1)}, u32[]{:S(2)}, u32[]{:S(2)}) collective-permute-start(bf16[128,768]{1,0:T(8,128)(2,1)} %get-tuple-element.223.other), channel_id=1, source_target_pairs={{0,24},{4,28},{8,16},{12,20},{16,8},{20,12},{24,0},{28,4},{1,25},{... | collective-permute-start | bytes 589832 | tf_op jit(solution)/shard_map/ppermute | solution.py:342
  15.3 23.1 %collective-permute-start.4 = (bf16[128,768]{1,0:T(8,128)(2,1)}, bf16[128,768]{1,0:T(8,128)(2,1)S(1)}, u32[]{:S(2)}, u32[]{:S(2)}) collective-permute-start(bf16[128,768]{1,0:T(8,128)(2,1)} %get-tuple-element.223.other), channel_id=1, source_target_pairs={{0,16},{4,20},{8,24},{12,28},{16,0},{20,4},{24,8},{28,12},{1,17},{... | collective-permute-start | bytes 589832 | tf_op jit(solution)/shard_map/ppermute | solution.py:342
  19.9 18.5 %collective-permute-start.3 = (bf16[128,768]{1,0:T(8,128)(2,1)}, bf16[128,768]{1,0:T(8,128)(2,1)S(1)}, u32[]{:S(2)}, u32[]{:S(2)}) collective-permute-start(bf16[128,768]{1,0:T(8,128)(2,1)} %get-tuple-element.242.mine), channel_id=1, source_target_pairs={{0,8},{4,12},{8,0},{12,4},{16,24},{20,28},{24,16},{28,20},{1,9},{5... | collective-permute-start | bytes 589832 | tf_op jit(solution)/shard_map/ppermute | solution.py:342
  27.4 23.5 %collective-permute-start.8 = (bf16[24,3840]{1,0:T(8,128)(2,1)}, bf16[24,3840]{1,0:T(8,128)(2,1)S(1)}, u32[]{:S(2)}, u32[]{:S(2)}) collective-permute-start(bf16[24,3840]{1,0:T(8,128)(2,1)} %get-tuple-element.228.p0), channel_id=1, source_target_pairs={{0,3},{1,2},{2,1},{3,0},{4,7},{5,6},{6,5},{7,4},{8,11},{9,10},{10,... | collective-permute-start | bytes 552968 | tf_op jit(solution)/shard_map/ppermute | solution.py:346
  29.2 21.8 %collective-permute-start.7 = (bf16[24,3840]{1,0:T(8,128)(2,1)}, bf16[24,3840]{1,0:T(8,128)(2,1)S(1)}, u32[]{:S(2)}, u32[]{:S(2)}) collective-permute-start(bf16[24,3840]{1,0:T(8,128)(2,1)} %get-tuple-element.228.p0), channel_id=1, source_target_pairs={{0,2},{1,3},{2,0},{3,1},{4,6},{5,7},{6,4},{7,5},{8,10},{9,11},{10,... | collective-permute-start | bytes 552968 | tf_op jit(solution)/shard_map/ppermute | solution.py:346
  41.5 18.2 %all-to-all-start.1 = ((bf16[8,96,576]{2,1,0:T(8,128)(2,1)}), bf16[8,96,576]{2,1,0:T(8,128)(2,1)S(1)}, u32[]{:S(2)}, u32[]{:S(2)}) async-start(bf16[8,96,576]{2,1,0:T(8,128)(2,1)} %attn_column.1), calls=%async_computation.1 | async-start | bytes 1966080 | tf_op jit(solution)/shard_map/all_to_all | solution.py:935
  59.7 19.4 %collective-permute-start.13 = (bf16[96,768]{1,0:T(8,128)(2,1)S(1)}, bf16[96,768]{1,0:T(8,128)(2,1)S(1)}, u32[]{:S(2)}, u32[]{:S(2)}) collective-permute-start(bf16[96,768]{1,0:T(8,128)(2,1)S(1)} %copy-done.33), channel_id=1, source_target_pairs={{0,3},{1,2},{2,1},{3,0},{4,7},{5,6},{6,5},{7,4},{8,11},{9,10},{10,... | collective-permute-start | bytes 442376 | tf_op jit(solution)/shard_map/ppermute | solution.py:346
  61.2 17.9 %collective-permute-start.12 = (bf16[96,768]{1,0:T(8,128)(2,1)S(1)}, bf16[96,768]{1,0:T(8,128)(2,1)S(1)}, u32[]{:S(2)}, u32[]{:S(2)}) collective-permute-start(bf16[96,768]{1,0:T(8,128)(2,1)S(1)} %copy-done.33), channel_id=1, source_target_pairs={{0,2},{1,3},{2,0},{3,1},{4,6},{5,7},{6,4},{7,5},{8,10},{9,11},{10,... | collective-permute-start | bytes 442376 | tf_op jit(solution)/shard_map/ppermute | solution.py:346
  63.1 16.0 %collective-permute-start.11 = (bf16[96,768]{1,0:T(8,128)(2,1)S(1)}, bf16[96,768]{1,0:T(8,128)(2,1)S(1)}, u32[]{:S(2)}, u32[]{:S(2)}) collective-permute-start(bf16[96,768]{1,0:T(8,128)(2,1)S(1)} %copy-done.33), channel_id=1, source_target_pairs={{0,1},{1,0},{2,3},{3,2},{4,5},{5,4},{6,7},{7,6},{8,9},{9,8},{10,11... | collective-permute-start | bytes 442376 | tf_op jit(solution)/shard_map/ppermute | solution.py:346
  64.1 18.5 %collective-permute-start.16 = (bf16[480,768]{1,0:T(8,128)(2,1)S(1)}, bf16[480,768]{1,0:T(8,128)(2,1)S(1)}, u32[]{:S(2)}, u32[]{:S(2)}) collective-permute-start(bf16[480,768]{1,0:T(8,128)(2,1)S(1)} %up_join.1.d0.u0), channel_id=1, source_target_pairs={{0,16},{4,20},{8,24},{12,28},{16,0},{20,4},{24,8},{28,12},{1,17},{... | collective-permute-start | bytes 2211848 | tf_op jit(solution)/shard_map/ppermute | solution.py:342
  64.6 17.9 %collective-permute-start.15 = (bf16[480,768]{1,0:T(8,128)(2,1)S(1)}, bf16[480,768]{1,0:T(8,128)(2,1)S(1)}, u32[]{:S(2)}, u32[]{:S(2)}) collective-permute-start(bf16[480,768]{1,0:T(8,128)(2,1)S(1)} %up_join.1.d0.u0), channel_id=1, source_target_pairs={{0,8},{4,12},{8,0},{12,4},{16,24},{20,28},{24,16},{28,20},{1,9},{5... | collective-permute-start | bytes 2211848 | tf_op jit(solution)/shard_map/ppermute | solution.py:342
  82.6 16.1 %collective-permute-start.21 = (bf16[240,768]{1,0:T(8,128)(2,1)S(1)}, bf16[240,768]{1,0:T(8,128)(2,1)S(1)}, u32[]{:S(2)}, u32[]{:S(2)}) collective-permute-start(bf16[240,768]{1,0:T(8,128)(2,1)S(1)} %slice.87), channel_id=1, source_target_pairs={{0,16},{4,20},{8,24},{12,28},{16,0},{20,4},{24,8},{28,12},{1,17},{... | collective-permute-start | bytes 1105928 | tf_op jit(solution)/shard_map/ppermute | solution.py:342
  84.1 14.7 %collective-permute-start.20 = (bf16[240,768]{1,0:T(8,128)(2,1)S(1)}, bf16[240,768]{1,0:T(8,128)(2,1)S(1)}, u32[]{:S(2)}, u32[]{:S(2)}) collective-permute-start(bf16[240,768]{1,0:T(8,128)(2,1)S(1)} %slice.86), channel_id=1, source_target_pairs={{0,8},{4,12},{8,0},{12,4},{16,24},{20,28},{24,16},{28,20},{1,9},{5... | collective-permute-start | bytes 1105928 | tf_op jit(solution)/shard_map/ppermute | solution.py:342
  99.5 15.7 %collective-permute-start.24 = (bf16[384,768]{1,0:T(8,128)(2,1)S(1)}, bf16[384,768]{1,0:T(8,128)(2,1)S(1)}, u32[]{:S(2)}, u32[]{:S(2)}) collective-permute-start(bf16[384,768]{1,0:T(8,128)(2,1)S(1)} %down_column.1.d0), channel_id=1, source_target_pairs={{0,16},{4,20},{8,24},{12,28},{16,0},{20,4},{24,8},{28,12},{1,17},{... | collective-permute-start | bytes 1769480 | tf_op jit(solution)/shard_map/ppermute | solution.py:342
  100.9 15.4 %collective-permute-start.23 = (bf16[384,768]{1,0:T(8,128)(2,1)S(1)}, bf16[384,768]{1,0:T(8,128)(2,1)S(1)}, u32[]{:S(2)}, u32[]{:S(2)}) collective-permute-start(bf16[384,768]{1,0:T(8,128)(2,1)S(1)} %down_column.1.d0), channel_id=1, source_target_pairs={{0,8},{4,12},{8,0},{12,4},{16,24},{20,28},{24,16},{28,20},{1,9},{5... | collective-permute-start | bytes 1769480 | tf_op jit(solution)/shard_map/ppermute | solution.py:342
  172.4 19.7 %collective-permute-start.42 = (bf16[192,768]{1,0:T(8,128)(2,1)S(1)}, bf16[192,768]{1,0:T(8,128)(2,1)S(1)}, u32[]{:S(2)}, u32[]{:S(2)}) collective-permute-start(bf16[192,768]{1,0:T(8,128)(2,1)S(1)} %get-tuple-element.348), channel_id=1, source_target_pairs={{0,8},{4,12},{8,0},{12,4},{16,24},{20,28},{24,16},{28,20},{1,9},{5... | collective-permute-start | bytes 884744 | tf_op jit(solution)/shard_map/ppermute | solution.py:342
  173.9 18.9 %collective-permute-start.43 = (bf16[192,768]{1,0:T(8,128)(2,1)S(1)}, bf16[192,768]{1,0:T(8,128)(2,1)S(1)}, u32[]{:S(2)}, u32[]{:S(2)}) collective-permute-start(bf16[192,768]{1,0:T(8,128)(2,1)S(1)} %get-tuple-element.349), channel_id=1, source_target_pairs={{0,16},{4,20},{8,24},{12,28},{16,0},{20,4},{24,8},{28,12},{1,17},{... | collective-permute-start | bytes 884744 | tf_op jit(solution)/shard_map/ppermute | solution.py:342
  174.5 19.1 %collective-permute-start.40 = (bf16[240,768]{1,0:T(8,128)(2,1)S(1)}, bf16[240,768]{1,0:T(8,128)(2,1)S(1)}, u32[]{:S(2)}, u32[]{:S(2)}) collective-permute-start(bf16[240,768]{1,0:T(8,128)(2,1)S(1)} %get-tuple-element.346), channel_id=1, source_target_pairs={{0,8},{4,12},{8,0},{12,4},{16,24},{20,28},{24,16},{28,20},{1,9},{5... | collective-permute-start | bytes 1105928 | tf_op jit(solution)/shard_map/ppermute | solution.py:342
  175.7 17.9 %collective-permute-start.41 = (bf16[240,768]{1,0:T(8,128)(2,1)S(1)}, bf16[240,768]{1,0:T(8,128)(2,1)S(1)}, u32[]{:S(2)}, u32[]{:S(2)}) collective-permute-start(bf16[240,768]{1,0:T(8,128)(2,1)S(1)} %get-tuple-element.347), channel_id=1, source_target_pairs={{0,16},{4,20},{8,24},{12,28},{16,0},{20,4},{24,8},{28,12},{1,17},{... | collective-permute-start | bytes 1105928 | tf_op jit(solution)/shard_map/ppermute | solution.py:342
  203.5 22.7 %collective-permute-start.46 = (bf16[480,768]{1,0:T(8,128)(2,1)}, bf16[480,768]{1,0:T(8,128)(2,1)}, u32[]{:S(2)}, u32[]{:S(2)}) collective-permute-start(bf16[480,768]{1,0:T(8,128)(2,1)} %get-tuple-element.372), channel_id=1, source_target_pairs={{0,8},{4,12},{8,0},{12,4},{16,24},{20,28},{24,16},{28,20},{1,9},{5... | collective-permute-start | bytes 2211848 | tf_op jit(solution)/shard_map/ppermute | solution.py:342
  205.0 21.2 %collective-permute-start.47 = (bf16[480,768]{1,0:T(8,128)(2,1)}, bf16[480,768]{1,0:T(8,128)(2,1)}, u32[]{:S(2)}, u32[]{:S(2)}) collective-permute-start(bf16[480,768]{1,0:T(8,128)(2,1)} %get-tuple-element.373), channel_id=1, source_target_pairs={{0,16},{4,20},{8,24},{12,28},{16,0},{20,4},{24,8},{28,12},{1,17},{... | collective-permute-start | bytes 2211848 | tf_op jit(solution)/shard_map/ppermute | solution.py:342
  207.8 18.4 %collective-permute-start.48 = (bf16[96,768]{1,0:T(8,128)(2,1)}, bf16[96,768]{1,0:T(8,128)(2,1)}, u32[]{:S(2)}, u32[]{:S(2)}) collective-permute-start(bf16[96,768]{1,0:T(8,128)(2,1)} %get-tuple-element.382), channel_id=1, source_target_pairs={{0,1},{1,0},{2,3},{3,2},{4,5},{5,4},{6,7},{7,6},{8,9},{9,8},{10,11... | collective-permute-start | bytes 442376 | tf_op jit(solution)/shard_map/ppermute | solution.py:346
  208.9 17.3 %collective-permute-start.49 = (bf16[96,768]{1,0:T(8,128)(2,1)}, bf16[96,768]{1,0:T(8,128)(2,1)}, u32[]{:S(2)}, u32[]{:S(2)}) collective-permute-start(bf16[96,768]{1,0:T(8,128)(2,1)} %get-tuple-element.383), channel_id=1, source_target_pairs={{0,2},{1,3},{2,0},{3,1},{4,6},{5,7},{6,4},{7,5},{8,10},{9,11},{10,... | collective-permute-start | bytes 442376 | tf_op jit(solution)/shard_map/ppermute | solution.py:346
  209.8 16.4 %collective-permute-start.50 = (bf16[96,768]{1,0:T(8,128)(2,1)}, bf16[96,768]{1,0:T(8,128)(2,1)}, u32[]{:S(2)}, u32[]{:S(2)}) collective-permute-start(bf16[96,768]{1,0:T(8,128)(2,1)} %get-tuple-element.384), channel_id=1, source_target_pairs={{0,3},{1,2},{2,1},{3,0},{4,7},{5,6},{6,5},{7,4},{8,11},{9,10},{10,... | collective-permute-start | bytes 442376 | tf_op jit(solution)/shard_map/ppermute | solution.py:346
  213.0 13.2 %all-to-all-start.2 = ((f32[32,1,312]{2,1,0:T(1,128)}), f32[32,1,312]{2,1,0:T(1,128)}, u32[]{:S(2)}, u32[]{:S(2)}) async-start(f32[32,1,312]{2,1,0:T(1,128)} %broadcast_in_dim.124), calls=%async_computation.2 | async-start | bytes 98304 | tf_op jit(solution)/shard_map/all_to_all | solution.py:1122
  226.2 13.8 %collective-permute-start.53 = (bf16[2,96,576]{2,1,0:T(8,128)(2,1)}, bf16[2,96,576]{2,1,0:T(8,128)(2,1)S(1)}, u32[]{:S(2)}, u32[]{:S(2)}) collective-permute-start(bf16[2,96,576]{2,1,0:T(8,128)(2,1)} %get-tuple-element.393), channel_id=1, source_target_pairs={{0,8},{4,12},{8,0},{12,4},{16,24},{20,28},{24,16},{28,20},{1,9},{5... | collective-permute-start | bytes 663560 | tf_op jit(solution)/shard_map/ppermute | solution.py:342
  240.8 15.7 %collective-permute-start.57 = (bf16[128,768]{1,0:T(8,128)(2,1)}, bf16[128,768]{1,0:T(8,128)(2,1)S(1)}, u32[]{:S(2)}, u32[]{:S(2)}) collective-permute-start(bf16[128,768]{1,0:T(8,128)(2,1)} %get-tuple-element.400), channel_id=1, source_target_pairs={{0,8},{4,12},{8,0},{12,4},{16,24},{20,28},{24,16},{28,20},{1,9},{5... | collective-permute-start | bytes 589832 | tf_op jit(solution)/shard_map/ppermute | solution.py:342
  241.6 14.8 %collective-permute-start.58 = (bf16[128,768]{1,0:T(8,128)(2,1)}, bf16[128,768]{1,0:T(8,128)(2,1)S(1)}, u32[]{:S(2)}, u32[]{:S(2)}) collective-permute-start(bf16[128,768]{1,0:T(8,128)(2,1)} %get-tuple-element.401), channel_id=1, source_target_pairs={{0,16},{4,20},{8,24},{12,28},{16,0},{20,4},{24,8},{28,12},{1,17},{... | collective-permute-start | bytes 589832 | tf_op jit(solution)/shard_map/ppermute | solution.py:342
  242.7 13.7 %collective-permute-start.51 = (bf16[120,768]{1,0:T(8,128)(2,1)}, bf16[120,768]{1,0:T(8,128)(2,1)}, u32[]{:S(2)}, u32[]{:S(2)}) collective-permute-start(bf16[120,768]{1,0:T(8,128)(2,1)} %get-tuple-element.391), channel_id=1, source_target_pairs={{0,2},{1,3},{2,0},{3,1},{4,6},{5,7},{6,4},{7,5},{8,10},{9,11},{10,... | collective-permute-start | bytes 552968 | tf_op jit(solution)/shard_map/ppermute | solution.py:346
  243.0 13.4 %collective-permute-start.52 = (bf16[120,768]{1,0:T(8,128)(2,1)}, bf16[120,768]{1,0:T(8,128)(2,1)}, u32[]{:S(2)}, u32[]{:S(2)}) collective-permute-start(bf16[120,768]{1,0:T(8,128)(2,1)} %get-tuple-element.392), channel_id=1, source_target_pairs={{0,3},{1,2},{2,1},{3,0},{4,7},{5,6},{6,5},{7,4},{8,11},{9,10},{10,... | collective-permute-start | bytes 552968 | tf_op jit(solution)/shard_map/ppermute | solution.py:346
  (87 other events, 617.6 us)
